TPU v7x, 32 devices: a whole 2x2x4 slice. The times are simulated.
32 devices in a mesh: grp: 2 (over y), gx: 4 (over z), gy: 4 (over x, core).
Axes of the slice: x: 2, y: 2, z: 4, core: 2. Of those that a mesh axis runs over, the one named last changes fastest.
Arguments:
- counts: int32 [256, 256, 256], P(('grp', 'gx'), 'gy'), parts along dimension 0, may hold values from -40 to 999
Outputs:
- denoised: float32 [256, 256, 256], P(('grp', 'gx'), 'gy'), parts along dimension 0
There are 2 independent parts, one for each index of `grp`. A program takes and returns all parts, laid end to end along the dimension named above; each array names one. Nothing has to cross between parts.
All inputs are finite; a program needn't handle non-finite values.
Results may differ from a plain program's by a relative error of at most 0.00005.
Values sent between devices are 32-bit elements; how exact they have to be, the bound alone decides.
A program may use at most 64 MiB of HBM per device.

v0:
```python
import functools
import math

import jax
import jax.numpy as jnp
import ml_dtypes
import numpy as np
from jax import lax
from jax.experimental import pallas as pl
from jax.experimental.pallas import tpu as pltpu
from jax.sharding import PartitionSpec as P

ROOT_THREE = math.sqrt(3.0)
TAP_SCALE = 4.0 * math.sqrt(2.0)
H = [
    (1.0 + ROOT_THREE) / TAP_SCALE,
    (3.0 + ROOT_THREE) / TAP_SCALE,
    (3.0 - ROOT_THREE) / TAP_SCALE,
    (1.0 - ROOT_THREE) / TAP_SCALE,
]
G = [H[3], -H[2], H[1], -H[0]]
THRESHOLD = 0.1
MESH = pl.DeviceIdType.MESH
F32 = jnp.float32
BF16 = jnp.bfloat16


def split_matrix(matrix):
    high = matrix.astype(ml_dtypes.bfloat16)
    low = (matrix - high.astype(np.float32)).astype(ml_dtypes.bfloat16)
    return np.stack([high, low])


def time_matrices(length, padded):
    matrix = np.zeros((padded, padded), np.float32)
    for k in range(length // 2):
        for j in range(4):
            matrix[(2 * k + j) % length, k] += H[j]
            matrix[(2 * k + j) % length, length // 2 + k] += G[j]
    return split_matrix(matrix), split_matrix(np.ascontiguousarray(matrix.T))


def times(values, matrix_ref):
    high = values.astype(BF16)
    low = (values - high.astype(F32)).astype(BF16)
    first, second = matrix_ref()
    dot = functools.partial(jnp.dot, preferred_element_type=F32)
    return dot(high, first) + (dot(low, first) + dot(high, second))


def shrink(values):
    return values - jnp.clip(values, -THRESHOLD, THRESHOLD)


def low_of(e):
    return (H[0] * e[0] + H[1] * e[1]) + (H[2] * e[2] + H[3] * e[3])


def high_of(e):
    return (G[0] * e[0] + G[1] * e[1]) + (G[2] * e[2] + G[3] * e[3])


def even_of(lo, hi, lo_before, hi_before):
    return (H[0] * lo + G[0] * hi) + (H[2] * lo_before + G[2] * hi_before)


def odd_of(lo, hi, lo_before, hi_before):
    return (H[1] * lo + G[1] * hi) + (H[3] * lo_before + G[3] * hi_before)


def loop(count, body, unroll=4):
    def step(i, carry):
        body(i)
        return carry

    lax.fori_loop(0, count, step, 0, unroll=unroll)


def rows(start, size):
    return pl.ds(pl.multiple_of(start, 8), size)


def kernel(
    nx, ny,
    counts_hbm, mats_hbm, out, counts, corner_counts, mats,
    t0, a0, c1, e1, t2, a2, c2, e2, t3, a3, c3,
    s3, p3, d2, s2, p2, d1, s1, p1, reb, edge, halo,
    f0x, f0y, f0c, f0xr, f0yr, f0cr,
    f1x, f1y, f1c, f1xr, f1yr, f1cr,
    i1x, i1y, i1c, i1xr, i1yr, i1cr,
    i2x, i2y, i2c, i2xr, i2yr, i2cr,
    local_sem, send_sem, recv_sem,
):
    gx = lax.axis_index("gx")
    gy = lax.axis_index("gy")
    x_after, x_before = lax.rem(gx + 1, nx), lax.rem(gx + nx - 1, nx)
    y_after, y_before = lax.rem(gy + 1, ny), lax.rem(gy + ny - 1, ny)
    before = [{"gx": x_before}, {"gy": y_before}, {"gx": x_before, "gy": y_before}]
    after = [{"gx": x_after}, {"gy": y_after}, {"gx": x_after, "gy": y_after}]

    loads = [
        pltpu.make_async_copy(source, target, local_sem.at[n])
        for n, (source, target) in enumerate(
            [
                (counts_hbm.at[:, 0:8, :], corner_counts),
                (counts_hbm.at[0:2], counts.at[0:2]),
                (mats_hbm, mats),
                (counts_hbm.at[2:32], counts.at[2:32]),
            ]
        )
    ]
    for load in loads:
        load.start()

    def matrix(first_row, size, first_column, width):
        return [
            mats[n, first_row : first_row + size, first_column : first_column + width]
            for n in range(2)
        ]

    barrier = pltpu.get_barrier_semaphore()
    for other in before + after:
        pl.semaphore_signal(barrier, inc=1, device_id=other, device_id_type=MESH)

    def send(round_no, sources, targets, others):
        copies = []
        for n in range(3):
            copy = pltpu.make_async_remote_copy(
                src_ref=sources[n],
                dst_ref=targets[n],
                send_sem=send_sem.at[3 * round_no + n],
                recv_sem=recv_sem.at[3 * round_no + n],
                device_id=others[n],
                device_id_type=MESH,
            )
            copy.start()
            copies.append(copy)
        return copies

    def wait(copies):
        for copy in copies:
            copy.wait()

    def residual(count, rebuilt):
        observed = count.astype(F32) * (1.0 / 64.0)
        weight = 1.0 / (1.0 + jnp.abs(observed))
        if rebuilt is None:
            return weight * observed
        return weight * (observed - rebuilt)

    def iteration(number):
        first = number == 0

        def old(ref, *index):
            return 0.0 if first else ref[index]

        m1 = functools.partial(matrix, 0, 256, 0, 256)
        m1t = functools.partial(matrix, 256, 256, 0, 256)
        m2 = functools.partial(matrix, 512, 128, 0, 128)
        m2t = functools.partial(matrix, 512, 128, 128, 128)
        m3 = functools.partial(matrix, 640, 128, 0, 128)
        m3t = functools.partial(matrix, 640, 128, 128, 128)

        if first:
            loads[0].wait()
            loads[1].wait()
        for i in range(2):
            for th in range(2):
                f0x[th, i * 64 : (i + 1) * 64, :] = residual(
                    counts[i, :, th * 128 : (th + 1) * 128],
                    None if first else reb[th, i * 64 : (i + 1) * 64, :],
                )

        def edge_row(x):
            for th in range(2):
                edge[th, rows(x * 8, 8), :] = residual(
                    corner_counts[x, :, th * 128 : (th + 1) * 128],
                    None if first else reb[th, rows(x * 64, 8), :],
                )

        loop(32, edge_row, unroll=4)
        for th in range(2):
            for j in range(2):
                f0y[th, j * 32 : (j + 1) * 32, :] = edge[th, pl.ds(j, 32, stride=8), :]
            for i in range(2):
                n = th * 8 + i * 4
                f0c[n : n + 4, :] = f0x[th, i * 64 : i * 64 + 4, :]
        if first:
            pl.semaphore_wait(barrier, 6)
        f0 = send(4 * number, [f0x, f0y, f0c], [f0xr, f0yr, f0cr], before)

        if first:
            loads[2].wait()
            loads[3].wait()

        def time_rows(n):
            count = counts[pl.ds(n * 4, 4)].reshape(256, 256)
            if first:
                values = residual(count, None)
            else:
                rebuilt = jnp.concatenate(
                    [reb[0, rows(n * 256, 256), :], reb[1, rows(n * 256, 256), :]], axis=1
                )
                values = residual(count, rebuilt)
            result = times(values, m1)
            for i in range(4):
                for tb in range(2):
                    t0[tb, rows((n * 4 + i) * 72, 64), :] = result[
                        i * 64 : (i + 1) * 64, tb * 128 : (tb + 1) * 128
                    ]

        loop(8, time_rows)
        wait(f0)
        result = times(jnp.concatenate([f0xr[0], f0xr[1]], axis=1), m1)
        for i in range(2):
            for tb in range(2):
                t0[tb, (32 + i) * 72 : (32 + i) * 72 + 64, :] = result[
                    i * 64 : (i + 1) * 64, tb * 128 : (tb + 1) * 128
                ]
        result = times(jnp.concatenate([f0yr[0], f0yr[1]], axis=1), m1)
        for j in range(2):
            for tb in range(2):
                t0[tb, pl.ds(64 + j, 32, stride=72), :] = result[
                    j * 32 : (j + 1) * 32, tb * 128 : (tb + 1) * 128
                ]
        result = times(jnp.concatenate([f0cr[0:8], f0cr[8:16]], axis=1), m1)
        for i in range(2):
            for tb in range(2):
                t0[tb, (32 + i) * 72 + 64 : (32 + i) * 72 + 66, :] = result[
                    i * 4 : i * 4 + 2, tb * 128 : (tb + 1) * 128
                ]

        def x_level1(k):
            for tb in range(2):
                e = [t0[tb, rows((2 * k + j) * 72, 72), :] for j in range(4)]
                a0[tb, rows(k * 72, 72), :] = low_of(e)
                a0[2 + tb, rows(k * 72, 72), :] = high_of(e)

        loop(16, x_level1)

        def y_level1(k):
            for xb in range(2):
                for tb in range(2):
                    e = [a0[2 * xb + tb, pl.ds(k * 72 + j, 32, stride=2), :] for j in range(4)]
                    for yb in range(2):
                        value = high_of(e) if yb else low_of(e)
                        band = 4 * xb + 2 * yb + tb
                        if band == 0:
                            e1[rows(k * 40, 32), :] = value
                        else:
                            place = rows((k + 1) * 40 + 8, 32)
                            c1[band - 1, place, :] = shrink(old(c1, band - 1, place, slice(None)) + value)

        loop(16, y_level1)

        for i in range(6):
            f1x[i * 32 : (i + 1) * 32, :] = e1[i * 40 : i * 40 + 32, :]
            f1c[i * 8 : (i + 1) * 8, :] = e1[i * 40 : i * 40 + 8, :]
            f1y[i * 16 : (i + 1) * 16, :] = e1[pl.ds(i, 16, stride=40), :]
        f1 = send(4 * number + 1, [f1x, f1y, f1c], [f1xr, f1yr, f1cr], before)
        for b in range(7):
            i1x[b * 32 : (b + 1) * 32, :] = c1[b, 16 * 40 + 8 : 17 * 40, :]
            i1y[b * 16 : (b + 1) * 16, :] = c1[b, pl.ds(40 + 39, 16, stride=40), :]
            i1c[b : b + 1, :] = c1[b, 17 * 40 - 1 : 17 * 40, :]
        i1c[7:8, :] = i1c[6:7, :]
        i1 = send(4 * number + 2, [i1x, i1y, i1c], [i1xr, i1yr, i1cr], after)

        def time_up1_own(n):
            place = rows(40 + n * 128, 128)
            for b in range(1, 4):
                values = jnp.concatenate([c1[2 * b - 1, place, :], c1[2 * b, place, :]], axis=1)
                result = times(values, m1t)
                s1[0, b, place, :] = result[:, :128]
                s1[1, b, place, :] = result[:, 128:]

        loop(5, time_up1_own)
        wait(f1)
        for i in range(6):
            e1[(16 + i) * 40 : (16 + i) * 40 + 32, :] = f1xr[i * 32 : (i + 1) * 32, :]
            e1[(16 + i) * 40 + 32 : (17 + i) * 40, :] = f1cr[i * 8 : (i + 1) * 8, :]
            e1[pl.ds(32 + i, 16, stride=40), :] = f1yr[i * 16 : (i + 1) * 16, :]

        def time_level2(n):
            t2[rows(n * 176, 176), :] = times(e1[rows(n * 176, 176), :], m2)

        loop(5, time_level2)

        def x_level2(k):
            e = [t2[rows((2 * k + j) * 40, 40), :] for j in range(4)]
            a2[0, rows(k * 40, 40), :] = low_of(e)
            a2[1, rows(k * 40, 40), :] = high_of(e)

        loop(10, x_level2)

        def y_level2_low(k):
            e = [a2[0, pl.ds(k * 40 + j, 18, stride=2), :] for j in range(4)]
            e2[rows(k * 24, 18), :] = low_of(e)

        loop(10, y_level2_low)

        def y_level2(k):
            place = rows((k + 2) * 24 + 8, 16)
            for xb in range(2):
                e = [a2[xb, pl.ds(k * 40 + j, 16, stride=2), :] for j in range(4)]
                for yb in range(2):
                    value = high_of(e) if yb else low_of(e)
                    b = 2 * xb + yb
                    c2[b, place, :] = shrink(old(c2, b, place, slice(None)) + value)

        loop(8, y_level2)

        t3[...] = times(e2[...], m3)

        def x_level3(k):
            e = [t3[rows((2 * k + j) * 24, 24), :] for j in range(4)]
            a3[0, rows(k * 24, 24), :] = low_of(e)
            a3[1, rows(k * 24, 24), :] = high_of(e)

        loop(4, x_level3)

        lane = lax.broadcasted_iota(jnp.int32, (8, 128), 1)

        def y_level3(k):
            place = rows((k + 2) * 16 + 8, 8)
            for xb in range(2):
                e = [a3[xb, pl.ds(k * 24 + j, 8, stride=2), :] for j in range(4)]
                for yb in range(2):
                    value = high_of(e) if yb else low_of(e)
                    b = 2 * xb + yb
                    value = old(c3, b, place, slice(None)) + value
                    if b == 0:
                        c3[b, place, :] = jnp.where(lane < 32, value, shrink(value))
                    else:
                        c3[b, place, :] = shrink(value)

        loop(4, y_level3)

        for b in range(4):
            for i in range(2):
                n = 2 * b + i
                i2x[n * 16 : (n + 1) * 16, :] = c2[b, (8 + i) * 24 + 8 : (9 + i) * 24, :]
                i2x[128 + n * 8 : 128 + (n + 1) * 8, :] = c3[b, (4 + i) * 16 + 8 : (5 + i) * 16, :]
                i2y[n * 8 : (n + 1) * 8, :] = c2[b, pl.ds(2 * 24 + 22 + i, 8, stride=24), :]
                i2y[64 + n * 4 : 64 + (n + 1) * 4, :] = c3[b, pl.ds(2 * 16 + 14 + i, 4, stride=16), :]
                i2c[n * 2 : n * 2 + 2, :] = c2[b, (9 + i) * 24 - 2 : (9 + i) * 24, :]
                i2c[16 + n * 2 : 18 + n * 2, :] = c3[b, (5 + i) * 16 - 2 : (5 + i) * 16, :]
        i2 = send(4 * number + 3, [i2x, i2y, i2c], [i2xr, i2yr, i2cr], after)

        wait(i1)
        c1[0, 8:40, :] = i1xr[0:32, :]
        c1[0, pl.ds(40 + 7, 16, stride=40), :] = i1yr[0:16, :]
        c1[0, 7:8, :] = i1cr[0:1, :]
        for b in range(1, 4):
            n = (b - 1) * 56
            for tb in range(2):
                d = 2 * b - 1 + tb
                halo[tb, n : n + 32, :] = i1xr[d * 32 : (d + 1) * 32, :]
                halo[tb, n + 32 : n + 48, :] = i1yr[d * 16 : (d + 1) * 16, :]
                halo[tb, n + 55 : n + 56, :] = i1cr[d : d + 1, :]
        result = times(jnp.concatenate([halo[0], halo[1]], axis=1), m1t)
        for b in range(1, 4):
            n = (b - 1) * 56
            for th in range(2):
                part = result[n : n + 56, th * 128 : (th + 1) * 128]
                s1[th, b, 8:40, :] = part[0:32]
                s1[th, b, pl.ds(40 + 7, 16, stride=40), :] = part[32:48]
                s1[th, b, 0:8, :] = part[48:56]

        def x_up1(yb, k):
            for th in range(2):
                e = [s1[th, b, rows((k + d) * 40, 40), :] for d in (1, 0) for b in (yb, 2 + yb)]
                p1[th, yb, rows(2 * k * 40, 40), :] = even_of(*e)
                p1[th, yb, rows((2 * k + 1) * 40, 40), :] = odd_of(*e)

        x_up1_low = functools.partial(x_up1, 0)
        x_up1_high = functools.partial(x_up1, 1)
        loop(16, x_up1_high)
        wait(i2)
        for b in range(4):
            for i in range(2):
                n = 2 * b + i
                c2[b, i * 24 + 8 : (i + 1) * 24, :] = i2xr[n * 16 : (n + 1) * 16, :]
                c3[b, i * 16 + 8 : (i + 1) * 16, :] = i2xr[128 + n * 8 : 128 + (n + 1) * 8, :]
                c2[b, pl.ds(2 * 24 + 6 + i, 8, stride=24), :] = i2yr[n * 8 : (n + 1) * 8, :]
                c3[b, pl.ds(2 * 16 + 6 + i, 4, stride=16), :] = i2yr[64 + n * 4 : 64 + (n + 1) * 4, :]
                c2[b, i * 24 + 6 : i * 24 + 8, :] = i2cr[n * 2 : n * 2 + 2, :]
                c3[b, i * 16 + 6 : i * 16 + 8, :] = i2cr[16 + n * 2 : 18 + n * 2, :]

        for b in range(4):
            s3[b] = times(c3[b], m3t)

        def x_up3(k):
            for yb in range(2):
                e = [s3[b, rows((k + d) * 16, 16), :] for d in (1, 0) for b in (yb, 2 + yb)]
                p3[yb, rows(2 * k * 16, 16), :] = even_of(*e)
                p3[yb, rows((2 * k + 1) * 16, 16), :] = odd_of(*e)

        loop(5, x_up3)

        def y_up3(r):
            e = [p3[b, pl.ds(r * 16 + d, 9), :] for d in (7, 6) for b in (0, 1)]
            d2[pl.ds(r * 24 + 6, 9, stride=2), :] = even_of(*e)
            d2[pl.ds(r * 24 + 7, 9, stride=2), :] = odd_of(*e)

        loop(10, y_up3)

        lanes = lax.broadcasted_iota(jnp.int32, (240, 128), 1)
        s2[0] = times(jnp.where(lanes < 64, d2[...], c2[0]), m2t)
        for b in range(1, 4):
            s2[b] = times(c2[b], m2t)

        def x_up2(k):
            for yb in range(2):
                e = [s2[b, rows((k + d) * 24, 24), :] for d in (1, 0) for b in (yb, 2 + yb)]
                p2[yb, rows(2 * k * 24, 24), :] = even_of(*e)
                p2[yb, rows((2 * k + 1) * 24, 24), :] = odd_of(*e)

        loop(9, x_up2)

        def y_up2(r):
            e = [p2[b, pl.ds(r * 24 + d, 17), :] for d in (7, 6) for b in (0, 1)]
            d1[pl.ds(r * 40 + 6, 17, stride=2), :] = even_of(*e)
            d1[pl.ds(r * 40 + 7, 17, stride=2), :] = odd_of(*e)

        loop(18, y_up2)

        def time_up1(n):
            place = rows(n * 136, 136)
            lo = d1[rows(40 + n * 136, 136), :]
            result = times(jnp.concatenate([lo, c1[0, place, :]], axis=1), m1t)
            s1[0, 0, place, :] = result[:, :128]
            s1[1, 0, place, :] = result[:, 128:]

        loop(5, time_up1)

        loop(16, x_up1_low)

        def y_up1(r):
            for th in range(2):
                e = [p1[th, b, pl.ds(r * 40 + d, 32), :] for d in (8, 7) for b in (0, 1)]
                reb[th, pl.ds(r * 64, 32, stride=2), :] = even_of(*e)
                reb[th, pl.ds(r * 64 + 1, 32, stride=2), :] = odd_of(*e)

        loop(32, y_up1)

    iteration(0)
    iteration(1)

    def finish(r):
        for th in range(2):
            out[r, :, th * 128 : (th + 1) * 128] = reb[th, rows(r * 64, 64), :]

    loop(32, finish, unroll=2)


def solution(mesh):
    nx, ny = mesh.shape["gx"], mesh.shape["gy"]
    m1, m1t = time_matrices(256, 256)
    m2, m2t = time_matrices(128, 128)
    m3, m3t = time_matrices(64, 128)

    mats = np.concatenate(
        [m1, m1t, np.concatenate([m2, m2t], axis=2), np.concatenate([m3, m3t], axis=2)], axis=1
    )

    def v(*shape):
        return pltpu.VMEM(shape, F32)

    scratch = [
        pltpu.VMEM((32, 64, 256), jnp.int32), pltpu.VMEM((32, 8, 256), jnp.int32),
        pltpu.VMEM(mats.shape, BF16),
        v(2, 34 * 72, 128), v(4, 16 * 72, 128), v(7, 17 * 40, 128), v(22 * 40, 128),
        v(22 * 40, 128), v(2, 10 * 40, 128), v(4, 10 * 24, 128), v(10 * 24, 128),
        v(10 * 24, 128), v(2, 4 * 24, 128), v(4, 6 * 16, 128),
        v(4, 6 * 16, 128), v(2, 10 * 16, 128), v(10 * 24, 128),
        v(4, 10 * 24, 128), v(2, 18 * 24, 128), v(18 * 40, 128),
        v(2, 4, 17 * 40, 128), v(2, 2, 32 * 40, 128), v(2, 32 * 64, 128), v(2, 32 * 8, 128),
        v(2, 168, 128),
    ]
    for shapes in (
        ((2, 128, 128), (2, 64, 128), (16, 128)),
        ((192, 128), (96, 128), (48, 128)),
        ((224, 128), (112, 128), (8, 128)),
        ((192, 128), (96, 128), (32, 128)),
    ):
        scratch += [v(*shape) for shape in shapes] * 2
    scratch += [pltpu.SemaphoreType.DMA((4,)), pltpu.SemaphoreType.DMA((24,)), pltpu.SemaphoreType.DMA((24,))]

    def on_device(counts):
        return pl.pallas_call(
            functools.partial(kernel, nx, ny),
            out_shape=jax.ShapeDtypeStruct(counts.shape, F32),
            in_specs=[pl.BlockSpec(memory_space=pltpu.HBM)] * 2,
            out_specs=pl.BlockSpec(memory_space=pltpu.VMEM),
            scratch_shapes=scratch,
            compiler_params=pltpu.CompilerParams(
                collective_id=0, has_side_effects=True, vmem_limit_bytes=50 * 1024 * 1024
            ),
        )(counts, mats)

    spec = P(("grp", "gx"), "gy", None)
    return jax.shard_map(on_device, mesh=mesh, in_specs=(spec,), out_specs=spec, check_vma=False)
```

profile of v0, /device:TPU:0, one launch (start us, length us, event | category | flops | bytes accessed | tf_op | source)
XLA Modules:
  0.0 50.6 jit_solution(10311630596811144834)
XLA Ops:
  0.0 0.0 copy-start
  0.0 1.1 %copy-done = bf16[2,768,256]{2,1,0:T(8,128)(2,1)S(1)} copy-done((bf16[2,768,256]{2,1,0:T(8,128)(2,1)S(1)}, bf16[2,768,256]{2,1,0:T(8,128)(2,1)}, u32[]{:S(2)}) %copy-start) | copy-done | bytes 786456
  1.1 48.1 %shard_map.28 = f32[32,64,256]{2,1,0:T(8,128)S(1)} custom-call(s32[32,64,256]{2,1,0:T(8,128)} %counts_hbm.1, bf16[2,768,256]{2,1,0:T(8,128)(2,1)S(1)} %copy-done), custom_call_target="tpu_custom_call" | custom-call | tf_op jit(solution)/shard_map/pallas_call | solution.py:490
  49.3 1.3 %copy.4 = f32[32,64,256]{2,1,0:T(8,128)} copy(f32[32,64,256]{2,1,0:T(8,128)S(1)} %shard_map.28) | data formatting | bytes 4194304
Async XLA Ops:
  0.0 1.1 %copy-start = (bf16[2,768,256]{2,1,0:T(8,128)(2,1)S(1)}, bf16[2,768,256]{2,1,0:T(8,128)(2,1)}, u32[]{:S(2)}) copy-start(bf16[2,768,256]{2,1,0:T(8,128)(2,1)} %constant.2.clone.mats_hbm) | copy-start | bytes 2359300
where the time goes:
time: 50.7 us; the launch traced here: 50.6 us
  Pallas kernels  48.1 us (95%)
  local copies, waits for them, and re-layouts  2.45 us (5%)
    pallas_call x1, Pallas kernels, on_device(): pl.pallas_call(functools.partial(kernel, nx, ny), out_shape=jax.ShapeDtyp...  48.1 us
    unnamed x3, local copies, waits for them, and re-layouts  2.45 us

commit v1 on v0

v1 whole, which is shorter than its diff:
```python
import functools
import math

import jax
import jax.numpy as jnp
from jax import lax
from jax.experimental import pallas as pl
from jax.experimental.pallas import tpu as pltpu
from jax.sharding import PartitionSpec as P

ROOT_THREE = math.sqrt(3.0)
TAP_SCALE = 4.0 * math.sqrt(2.0)
H = [
    (1.0 + ROOT_THREE) / TAP_SCALE,
    (3.0 + ROOT_THREE) / TAP_SCALE,
    (3.0 - ROOT_THREE) / TAP_SCALE,
    (1.0 - ROOT_THREE) / TAP_SCALE,
]
G = [H[3], -H[2], H[1], -H[0]]
RATIO = 2.0 - ROOT_THREE
SPATIAL_SCALE = H[0] * H[0]
THRESHOLD = 0.1
MESH = pl.DeviceIdType.MESH
F32 = jnp.float32
BF16 = jnp.bfloat16

PLACES = [36, 39, 0, 2, 3, 38]


def shrink(values):
    return values - jnp.clip(values, -THRESHOLD, THRESHOLD)


def p_of(even, odd):
    return even + ROOT_THREE * odd


def q_of(even, odd):
    return ROOT_THREE * even - odd


def q_even(even, odd):
    return even - (1.0 / ROOT_THREE) * odd


def low_of(p, q_after):
    return p + RATIO * q_after


def high_of(p, q_after):
    return q_after - RATIO * p


def loop(count, body, unroll=4):
    def step(i, carry):
        body(i)
        return carry

    lax.fori_loop(0, count, step, 0, unroll=unroll)


def rows(start, size):
    return pl.ds(pl.multiple_of(start, 8), size)


def build_matrix(ref, length, padded, transposed):
    t = lax.broadcasted_iota(jnp.int32, (padded, padded), 1 if transposed else 0)
    c = lax.broadcasted_iota(jnp.int32, (padded, padded), 0 if transposed else 1)
    half = c >= length // 2
    j = (t - 2 * jnp.where(half, c - length // 2, c)) & (length - 1)
    value = jnp.zeros((padded, padded), F32)
    for tap in range(4):
        tap_value = jnp.where(half, G[tap] * SPATIAL_SCALE, H[tap] * SPATIAL_SCALE)
        value = jnp.where(j == tap, tap_value, value)
    if padded > length:
        value = jnp.where((t < length) & (c < length), value, 0.0)
    high = value.astype(BF16)
    low = (value - high.astype(F32)).astype(BF16)
    ref[0:padded, :] = high
    ref[padded : 2 * padded, :] = high
    ref[2 * padded : 3 * padded, :] = low


def times(values, matrix_ref):
    high = values.astype(BF16)
    low = (values - high.astype(F32)).astype(BF16)
    left = jnp.concatenate([high, low, high], axis=1)
    return jnp.dot(left, matrix_ref[...], preferred_element_type=F32)


def functionals(entry, count, q_last):
    def low2(i):
        return low_of(p_of(entry(i), entry(i + 1)), q_of(entry(i + 2), entry(i + 3)))

    n = count - 8
    return [
        q_last(entry(0), entry(1)),
        q_last(low2(0), low2(2)),
        p_of(entry(n + 4), entry(n + 5)),
        entry(n + 6),
        entry(n + 7),
        p_of(low2(n), low2(n + 2)),
    ]


def kernel(
    nx, ny,
    counts_hbm, out, counts, m1, m1t, m2, m2t, m3, m3t,
    t0, c1, e1, t2, a2, c2, e2, t3, a3, c3,
    s3, p3, d2, s2, p2, d1, s1, reb, halo,
    f0x, f0y, f0c, f0yr, f0cr,
    f1x, f1y, f1xr, f1yr,
    i1x, i1y, i1c, i1xr, i1yr, i1cr,
    local_sem, send_sem, recv_sem,
):
    gx = lax.axis_index("gx")
    gy = lax.axis_index("gy")

    def device(dx, dy):
        where = {}
        if dx:
            where["gx"] = lax.rem(gx + dx + nx, nx)
        if dy:
            where["gy"] = lax.rem(gy + dy + ny, ny)
        return where

    load = pltpu.make_async_copy(counts_hbm, counts, local_sem.at[0])
    load.start()

    barrier = pltpu.get_barrier_semaphore()
    around = [(dx, dy) for dx in (-1, 0, 1) for dy in (-1, 0, 1) if dx or dy]
    for dx, dy in around:
        pl.semaphore_signal(barrier, inc=1, device_id=device(dx, dy), device_id_type=MESH)

    def send(first_sem, transfers):
        copies = []
        for n, (source, target, dx, dy) in enumerate(transfers):
            copy = pltpu.make_async_remote_copy(
                src_ref=source,
                dst_ref=target,
                send_sem=send_sem.at[first_sem + n],
                recv_sem=recv_sem.at[first_sem + n],
                device_id=device(dx, dy),
                device_id_type=MESH,
            )
            copy.start()
            copies.append(copy)
        return copies

    def wait(copies):
        for copy in copies:
            copy.wait()

    build_matrix(m1, 256, 256, False)
    build_matrix(m1t, 256, 256, True)
    build_matrix(m2, 128, 128, False)
    build_matrix(m2t, 128, 128, True)
    build_matrix(m3, 64, 128, False)
    build_matrix(m3t, 64, 128, True)
    for tb in range(2):
        t0[tb, pl.ds(65, 33, stride=72), :] = jnp.zeros((33, 128), F32)
    for place in (1, 37):
        e1[pl.ds(place, 22, stride=40), :] = jnp.zeros((22, 128), F32)
    for place in (1, 21):
        e2[pl.ds(place, 12, stride=24), :] = jnp.zeros((12, 128), F32)
    for b in range(7):
        c1[b, 0:40, :] = jnp.zeros((40, 128), F32)
        c1[b, pl.ds(47, 16, stride=40), :] = jnp.zeros((16, 128), F32)
    for th in range(2):
        for b in range(1, 4):
            s1[th, b, 0:40, :] = jnp.zeros((40, 128), F32)
    f0c[...] = jnp.zeros((8, 128), F32)
    i1c[...] = jnp.zeros((8, 128), F32)
    f1y[...] = jnp.zeros((6, 32, 128), F32)
    load.wait()

    def residual(count, rebuilt):
        observed = count.astype(F32) * (1.0 / 64.0)
        weight = 1.0 / (1.0 + jnp.abs(observed))
        if rebuilt is None:
            return weight * observed
        return weight * (observed - rebuilt)

    def iteration(number):
        first = number == 0
        sem = 14 * number

        def old(ref, *index):
            return 0.0 if first else ref[index]

        def time_rows(n):
            count = counts[pl.ds(n * 4, 4)].reshape(256, 256)
            if first:
                values = residual(count, None)
            else:
                rebuilt = jnp.concatenate(
                    [reb[0, rows(n * 256, 256), :], reb[1, rows(n * 256, 256), :]], axis=1
                )
                values = residual(count, rebuilt)
            result = times(values, m1)
            for i in range(4):
                for tb in range(2):
                    t0[tb, rows((n * 4 + i) * 72, 64), :] = result[
                        i * 64 : (i + 1) * 64, tb * 128 : (tb + 1) * 128
                    ]

        loop(8, time_rows)

        for tb in range(2):
            f0x[tb] = q_of(t0[tb, 0:64, :], t0[tb, 72:136, :])
            f0y[tb] = q_even(t0[tb, pl.ds(0, 32, stride=72), :], t0[tb, pl.ds(1, 32, stride=72), :])
            f0c[tb : tb + 1, :] = q_even(f0x[tb, 0:1, :], f0x[tb, 1:2, :])
        if first:
            pl.semaphore_wait(barrier, 8)
        f0 = send(sem, [
            (f0x, t0.at[:, 2304:2368, :], -1, 0),
            (f0y, f0yr, 0, -1),
            (f0c, f0cr, -1, -1),
        ])

        def y_level1(row, chunk, tb):
            e = [t0[tb, pl.ds(row * 72 + 16 * chunk + j, 8, stride=2), :] for j in range(4)]
            p, q = p_of(e[0], e[1]), q_of(e[2], e[3])
            return [low_of(p, q), high_of(p, q)]

        def level1_store(k, chunk, tb, yb, p, q):
            for xb in range(2):
                value = high_of(p, q) if xb else low_of(p, q)
                band = 4 * xb + 2 * yb + tb
                if band == 0:
                    e1[pl.ds((k + 4) * 40 + 4 + 8 * chunk, 8), :] = value
                else:
                    place = rows((k + 1) * 40 + 8 + 8 * chunk, 8)
                    c1[band - 1, place, :] = shrink(old(c1, band - 1, place, slice(None)) + value)

        def level1(chunks):
            parts = [(chunk, tb) for chunk in chunks for tb in range(2)]

            def pair(k):
                result = []
                for chunk, tb in parts:
                    first_row = y_level1(2 * k, chunk, tb)
                    second_row = y_level1(2 * k + 1, chunk, tb)
                    for yb in range(2):
                        result.append((first_row[yb], second_row[yb]))
                return result

            def step(i, ps):
                k = i + 1
                after = pair(k)
                n = 0
                for chunk, tb in parts:
                    for yb in range(2):
                        level1_store(i, chunk, tb, yb, ps[n], q_of(*after[n]))
                        n += 1
                return tuple(p_of(*one) for one in after)

            return lax.fori_loop(0, 15, step, tuple(p_of(*one) for one in pair(0)), unroll=3)

        def level1_last(chunks, ps):
            n = 0
            for chunk in chunks:
                for tb in range(2):
                    halo_row = y_level1(32, chunk, tb)
                    for yb in range(2):
                        level1_store(15, chunk, tb, yb, ps[n], halo_row[yb])
                        n += 1

        inner = level1((0, 1, 2))
        wait(f0)
        for tb in range(2):
            t0[tb, pl.ds(64, 32, stride=72), :] = f0yr[tb]
            t0[tb, 2368:2369, :] = f0cr[tb : tb + 1, :]
        level1_last((0, 1, 2), inner)
        level1_last((3,), level1((3,)))

        for n, value in enumerate(
            functionals(lambda i: e1[(4 + i) * 40 + 4 : (4 + i) * 40 + 36, :], 16, q_of)
        ):
            f1x[n * 32 : (n + 1) * 32, :] = value
        for start, size, stride, target, offset in ((164, 16, 40, 0, e1), (0, 2, 32, 16, f1x), (64, 4, 32, 24, f1x)):
            for n, value in enumerate(
                functionals(lambda i: offset[pl.ds(start + i, size, stride=stride), :], 32, q_even)
            ):
                f1y[n, target : target + size, :] = value
        xr, yr = f1xr.at[number], f1yr.at[number]
        f1 = send(sem + 3, [
            (f1x.at[0:64], xr.at[0:64], -1, 0),
            (f1x.at[64:192], xr.at[64:192], 1, 0),
            (f1y.at[0:2, 0:16], yr.at[0:2, 0:16], 0, -1),
            (f1y.at[2:6, 0:16], yr.at[2:6, 0:16], 0, 1),
            (f1y.at[0:2, 16:24], yr.at[0:2, 16:24], -1, -1),
            (f1y.at[2:6, 16:24], yr.at[2:6, 16:24], -1, 1),
            (f1y.at[0:2, 24:32], yr.at[0:2, 24:32], 1, -1),
            (f1y.at[2:6, 24:32], yr.at[2:6, 24:32], 1, 1),
        ])

        def i1_rows(read):
            bands = [read(b) for b in range(7)]
            return bands, [bands[3], bands[4] + RATIO * bands[0], bands[5] + RATIO * bands[1], bands[6] + RATIO * bands[2]]

        _, values = i1_rows(lambda b: c1[b, 648:680, :])
        for n in range(4):
            i1x[n * 32 : (n + 1) * 32, :] = values[n]
        bands, _ = i1_rows(lambda b: c1[b, pl.ds(79, 16, stride=40), :])
        values = [bands[1], bands[2] + RATIO * bands[0], bands[5] + RATIO * bands[3], bands[6] + RATIO * bands[4]]
        for n in range(4):
            i1y[n * 16 : (n + 1) * 16, :] = values[n]
        _, values = i1_rows(lambda b: c1[b, 679:680, :])
        for n in range(2):
            i1c[n : n + 1, :] = RATIO * values[n] + values[2 + n]
        i1 = send(sem + 11, [(i1x, i1xr, 1, 0), (i1y, i1yr, 0, 1), (i1c, i1cr, 1, 1)])

        def time_up1_own(n):
            place = rows(40 + n * 128, 128)
            for b in range(1, 4):
                values = jnp.concatenate([c1[2 * b - 1, place, :], c1[2 * b, place, :]], axis=1)
                result = times(values, m1t)
                s1[0, b, place, :] = result[:, :128]
                s1[1, b, place, :] = result[:, 128:]

        loop(5, time_up1_own, unroll=5)
        wait(f1)
        e1[804:836, :] = xr[0:32, :]
        e1[844:876, :] = xr[32:64, :]
        for n in range(4):
            e1[n * 40 + 4 : n * 40 + 36, :] = xr[64 + n * 32 : 96 + n * 32, :]
        for n, place in enumerate(PLACES):
            e1[pl.ds(160 + place, 16, stride=40), :] = yr[n, 0:16, :]
            e1[pl.ds(800 + place, 2, stride=40), :] = yr[n, 16:18, :]
            e1[pl.ds(place, 4, stride=40), :] = yr[n, 24:28, :]

        def time_level2(n):
            t2[rows(n * 176, 176), :] = times(e1[rows(n * 176, 176), :], m2)

        loop(5, time_level2, unroll=5)

        def pairs(row, before, first_pair, count, last):
            ps = [row(before), p_of(row(first_pair), row(first_pair + 1))]
            qs = [q_of(row(first_pair), row(first_pair + 1))]
            return ps, qs

        def t2_row(i):
            return t2[i * 40 : (i + 1) * 40, :]

        p_now, q_after = t2_row(0), None
        for k in range(-2, 8):
            if k == 7:
                q_after, p_after = t2_row(20), None
            else:
                m = 1 if k == -2 else 6 + 2 * k
                even, odd = t2_row(m), t2_row(m + 1)
                q_after, p_after = q_of(even, odd), p_of(even, odd)
            n = (k + 2) * 40
            a2[0, n : n + 40, :] = low_of(p_now, q_after)
            a2[1, n : n + 40, :] = high_of(p_now, q_after)
            p_now = p_after
        a2[0, 400:440, :] = t2_row(3)
        a2[0, 440:480, :] = t2_row(21)

        def y_level2_of(xb, k):
            e = [a2[xb, pl.ds(k * 40 + j, 18, stride=2), :] for j in range(4)]
            return p_of(e[0], e[1]), q_of(e[2], e[3])

        def y_level2(k):
            place = rows(k * 24, 18)
            for xb in range(2):
                p, q = y_level2_of(xb, k)
                for yb in range(2):
                    value = high_of(p, q) if yb else low_of(p, q)
                    b = 2 * xb + yb
                    if b == 0:
                        e2[pl.ds(k * 24 + 2, 18), :] = value
                    c2[b, place, :] = shrink(old(c2, b, place, slice(None)) + value)

        def y_level2_low(k):
            e2[pl.ds(k * 24 + 2, 18), :] = low_of(*y_level2_of(0, k))

        for k in range(10, 12):
            y_level2_low(k)
        loop(10, y_level2, unroll=10)
        for source, target in ((38, 0), (39, 20)):
            e2[pl.ds(target, 12, stride=24), :] = a2[0, pl.ds(source, 12, stride=40), :]

        t3[...] = times(e2[...], m3)

        def t3_row(i):
            return t3[i * 24 : (i + 1) * 24, :]

        p_now = t3_row(10)
        for k in range(-2, 4):
            if k == 3:
                q_after, p_after = t3_row(11), None
            else:
                even, odd = t3_row(2 * k + 4), t3_row(2 * k + 5)
                q_after, p_after = q_of(even, odd), p_of(even, odd)
            n = (k + 2) * 24
            a3[0, n : n + 24, :] = low_of(p_now, q_after)
            a3[1, n : n + 24, :] = high_of(p_now, q_after)
            p_now = p_after

        lane = lax.broadcasted_iota(jnp.int32, (10, 128), 1)

        def y_level3(k):
            place = rows(k * 16, 10)
            for xb in range(2):
                e = [a3[xb, pl.ds(k * 24 + j, 10, stride=2), :] for j in range(4)]
                p, q = p_of(e[0], e[1]), q_of(e[2], e[3])
                for yb in range(2):
                    value = high_of(p, q) if yb else low_of(p, q)
                    b = 2 * xb + yb
                    value = old(c3, b, place, slice(None)) + value
                    if b == 0:
                        c3[b, place, :] = jnp.where(lane < 32, value, shrink(value))
                    else:
                        c3[b, place, :] = shrink(value)

        loop(6, y_level3, unroll=6)

        def up(low_now, high_now, low_before, high_before):
            p = low_now - RATIO * high_now
            q = high_before + RATIO * low_before
            return p + ROOT_THREE * q, ROOT_THREE * p - q

        for b in range(4):
            s3[b] = times(c3[b], m3t)

        def x_up3(k):
            for yb in range(2):
                e = [s3[b, rows((k + d) * 16, 16), :] for d in (1, 0) for b in (yb, 2 + yb)]
                even, odd = up(*e)
                p3[yb, rows(2 * k * 16, 16), :] = even
                p3[yb, rows((2 * k + 1) * 16, 16), :] = odd

        loop(5, x_up3, unroll=5)

        def y_up3(r):
            e = [p3[b, pl.ds(r * 16 + d, 9), :] for d in (1, 0) for b in (0, 1)]
            even, odd = up(*e)
            d2[pl.ds(r * 24, 9, stride=2), :] = even
            d2[pl.ds(r * 24 + 1, 9, stride=2), :] = odd

        loop(10, y_up3, unroll=10)

        lanes = lax.broadcasted_iota(jnp.int32, (240, 128), 1)
        for b in range(1, 4):
            s2[b] = times(c2[b], m2t)
        s2[0] = times(jnp.where(lanes < 64, d2[...], c2[0]), m2t)

        def x_up2(k):
            for yb in range(2):
                e = [s2[b, rows((k + d) * 24, 24), :] for d in (1, 0) for b in (yb, 2 + yb)]
                even, odd = up(*e)
                p2[yb, rows(2 * k * 24, 24), :] = even
                p2[yb, rows((2 * k + 1) * 24, 24), :] = odd

        loop(9, x_up2, unroll=9)

        def y_up2(r):
            e = [p2[b, pl.ds(r * 24 + d, 17), :] for d in (1, 0) for b in (0, 1)]
            even, odd = up(*e)
            d1[pl.ds(r * 40 + 6, 17, stride=2), :] = even
            d1[pl.ds(r * 40 + 7, 17, stride=2), :] = odd

        loop(18, y_up2, unroll=6)

        wait(i1)
        for tb in range(2):
            halo[tb, 0:32, :] = i1xr[tb * 32 : (tb + 1) * 32, :]
            halo[tb, 32:64, :] = i1xr[(2 + tb) * 32 : (3 + tb) * 32, :]
            halo[tb, 64:80, :] = i1yr[tb * 16 : (tb + 1) * 16, :]
            halo[tb, 80:96, :] = i1yr[(2 + tb) * 16 : (3 + tb) * 16, :]
            halo[tb, 96:97, :] = i1cr[tb : tb + 1, :]
        result = times(jnp.concatenate([halo[0], halo[1]], axis=1), m1t)
        for th in range(2):
            part = result[:, th * 128 : (th + 1) * 128]
            s1[th, 2, 8:40, :] = part[0:32]
            s1[th, 3, 8:40, :] = part[32:64]
            s1[th, 1, pl.ds(47, 16, stride=40), :] = part[64:80]
            s1[th, 3, pl.ds(47, 16, stride=40), :] = part[80:96]
            s1[th, 3, 7:8, :] = part[96:97]

        def time_up1(n):
            place = rows(n * 136, 136)
            lo = d1[rows(40 + n * 136, 136), :]
            result = times(jnp.concatenate([lo, c1[0, place, :]], axis=1), m1t)
            s1[0, 0, place, :] = result[:, :128]
            s1[1, 0, place, :] = result[:, 128:]

        loop(5, time_up1, unroll=5)

        up_parts = [(chunk, th) for chunk in range(4) for th in range(2)]

        def y_up1(row, chunk, th):
            result = []
            for xb in range(2):
                e = [
                    s1[th, 2 * xb + yb, pl.ds(row * 40 + d + 8 * chunk, 8), :]
                    for d in (8, 7) for yb in range(2)
                ]
                result.append(up(*e))
            return [(result[0][n], result[1][n]) for n in range(2)]

        def q_next(low, high):
            return high + RATIO * low

        def up1(k, qs):
            after = []
            n = 0
            for chunk, th in up_parts:
                for parity, (low, high) in enumerate(y_up1(k + 1, chunk, th)):
                    p = low - RATIO * high
                    start = k * 128 + 16 * chunk + parity
                    reb[th, pl.ds(start, 8, stride=2), :] = p + ROOT_THREE * qs[n]
                    reb[th, pl.ds(start + 64, 8, stride=2), :] = ROOT_THREE * p - qs[n]
                    after.append(q_next(low, high))
                    n += 1
            return tuple(after)

        start = tuple(q_next(*one) for chunk, th in up_parts for one in y_up1(0, chunk, th))
        lax.fori_loop(0, 16, up1, start, unroll=2)

    iteration(0)
    iteration(1)

    def finish(r):
        for th in range(2):
            out[r, :, th * 128 : (th + 1) * 128] = reb[th, rows(r * 64, 64), :]

    loop(32, finish, unroll=2)


def solution(mesh):
    nx, ny = mesh.shape["gx"], mesh.shape["gy"]

    def v(*shape):
        return pltpu.VMEM(shape, F32)

    def b(*shape):
        return pltpu.VMEM(shape, BF16)

    scratch = [
        pltpu.VMEM((32, 64, 256), jnp.int32),
        b(768, 256), b(768, 256), b(384, 128), b(384, 128), b(384, 128), b(384, 128),
        v(2, 33 * 72, 128), v(7, 17 * 40, 128), v(22 * 40, 128),
        v(22 * 40, 128), v(2, 12 * 40, 128), v(4, 10 * 24, 128), v(12 * 24, 128),
        v(12 * 24, 128), v(2, 6 * 24, 128), v(4, 6 * 16, 128),
        v(4, 6 * 16, 128), v(2, 10 * 16, 128), v(10 * 24, 128),
        v(4, 10 * 24, 128), v(2, 18 * 24, 128), v(18 * 40, 128),
        v(2, 4, 17 * 40, 128), v(2, 32 * 64, 128), v(2, 104, 128),
        v(2, 64, 128), v(2, 32, 128), v(8, 128), v(2, 32, 128), v(8, 128),
        v(192, 128), v(6, 32, 128), v(2, 192, 128), v(2, 6, 32, 128),
        v(128, 128), v(64, 128), v(8, 128), v(128, 128), v(64, 128), v(8, 128),
        pltpu.SemaphoreType.DMA((1,)), pltpu.SemaphoreType.DMA((28,)), pltpu.SemaphoreType.DMA((28,)),
    ]

    def on_device(counts):
        return pl.pallas_call(
            functools.partial(kernel, nx, ny),
            out_shape=jax.ShapeDtypeStruct(counts.shape, F32),
            in_specs=[pl.BlockSpec(memory_space=pltpu.HBM)],
            out_specs=pl.BlockSpec(memory_space=pltpu.VMEM),
            scratch_shapes=scratch,
            compiler_params=pltpu.CompilerParams(
                collective_id=0, has_side_effects=True, vmem_limit_bytes=50 * 1024 * 1024
            ),
        )(counts)

    spec = P(("grp", "gx"), "gy", None)
    return jax.shard_map(on_device, mesh=mesh, in_specs=(spec,), out_specs=spec, check_vma=False)
```

time: 50.7 us -> 37.2 us (0.73)
  Pallas kernels: 48.1 us -> 35.7 us
  local copies, waits for them, and re-layouts: 2.45 us -> 1.32 us
    pallas_call x1, Pallas kernels: 48.1 us -> 35.7 us  [on_device(): pl.pallas_call(functools.partial(kernel, nx, ny), out_shape=jax.ShapeDtyp...]
    unnamed x3 -> x1, local copies, waits for them, and re-layouts: 2.45 us -> 1.32 us
where the time goes in v1:
time: 37.2 us; the launch traced here: 37.1 us
  Pallas kernels  35.7 us (96%)
  local copies, waits for them, and re-layouts  1.32 us (4%)
    pallas_call x1, Pallas kernels, on_device(): pl.pallas_call(functools.partial(kernel, nx, ny), out_shape=jax.ShapeDtyp...  35.7 us
    unnamed x1, local copies, waits for them, and re-layouts  1.32 us

profile of v1, /device:TPU:0, one launch (start us, length us, event | category | flops | bytes accessed | tf_op | source)
XLA Modules:
  0.0 37.1 jit_solution(6832031143132684725)
XLA Ops:
  0.0 35.7 %shard_map.17 = f32[32,64,256]{2,1,0:T(8,128)S(1)} custom-call(s32[32,64,256]{2,1,0:T(8,128)} %counts_hbm.1), custom_call_target="tpu_custom_call" | custom-call | tf_op jit(solution)/shard_map/pallas_call | solution.py:558
  35.8 1.3 %copy.3 = f32[32,64,256]{2,1,0:T(8,128)} copy(f32[32,64,256]{2,1,0:T(8,128)S(1)} %shard_map.17) | data formatting | bytes 4194304

commit v2 on v1

--- a/solution.py
+++ b/solution.py
@@ -24,7 +24,7 @@
 F32 = jnp.float32
 BF16 = jnp.bfloat16
 
-PLACES = [36, 39, 0, 2, 3, 38]
+PLACES = [36, 39, 37, 0, 2, 3, 38]
 
 
 def shrink(values):
@@ -88,7 +88,7 @@
     return jnp.dot(left, matrix_ref[...], preferred_element_type=F32)
 
 
-def functionals(entry, count, q_last):
+def functionals(entry, count, level1_q, q_last):
     def low2(i):
         return low_of(p_of(entry(i), entry(i + 1)), q_of(entry(i + 2), entry(i + 3)))
 
@@ -96,6 +96,7 @@
     return [
         q_last(entry(0), entry(1)),
         q_last(low2(0), low2(2)),
+        level1_q,
         p_of(entry(n + 4), entry(n + 5)),
         entry(n + 6),
         entry(n + 7),
@@ -107,10 +108,9 @@
     nx, ny,
     counts_hbm, out, counts, m1, m1t, m2, m2t, m3, m3t,
     t0, c1, e1, t2, a2, c2, e2, t3, a3, c3,
-    s3, p3, d2, s2, p2, d1, s1, reb, halo,
-    f0x, f0y, f0c, f0yr, f0cr,
+    s3, p3, d2, s2, p2, d1, s1, reb, cb,
+    f0q, f0p, f0y, f0qr, f0pr, f0yr,
     f1x, f1y, f1xr, f1yr,
-    i1x, i1y, i1c, i1xr, i1yr, i1cr,
     local_sem, send_sem, recv_sem,
 ):
     gx = lax.axis_index("gx")
@@ -157,21 +157,23 @@
     build_matrix(m2t, 128, 128, True)
     build_matrix(m3, 64, 128, False)
     build_matrix(m3t, 64, 128, True)
+    for ref in (f0q, f0p):
+        for tb in range(2):
+            ref[tb, 64:72, :] = jnp.zeros((8, 128), F32)
+    for ref in (f0qr, f0pr):
+        for number in range(2):
+            for tb in range(2):
+                ref[number, tb, 64:72, :] = jnp.zeros((8, 128), F32)
+    for n in range(4):
+        f0y[n, 32:40, :] = jnp.zeros((8, 128), F32)
+        for place in (1, 35):
+            cb[n, place : place + 1, :] = jnp.zeros((1, 128), F32)
     for tb in range(2):
-        t0[tb, pl.ds(65, 33, stride=72), :] = jnp.zeros((33, 128), F32)
-    for place in (1, 37):
-        e1[pl.ds(place, 22, stride=40), :] = jnp.zeros((22, 128), F32)
+        t0[tb, pl.ds(65, 32, stride=72), :] = jnp.zeros((32, 128), F32)
     for place in (1, 21):
         e2[pl.ds(place, 12, stride=24), :] = jnp.zeros((12, 128), F32)
-    for b in range(7):
-        c1[b, 0:40, :] = jnp.zeros((40, 128), F32)
-        c1[b, pl.ds(47, 16, stride=40), :] = jnp.zeros((16, 128), F32)
-    for th in range(2):
-        for b in range(1, 4):
-            s1[th, b, 0:40, :] = jnp.zeros((40, 128), F32)
-    f0c[...] = jnp.zeros((8, 128), F32)
-    i1c[...] = jnp.zeros((8, 128), F32)
-    f1y[...] = jnp.zeros((6, 32, 128), F32)
+    e1[...] = jnp.zeros((960, 128), F32)
+    f1y[...] = jnp.zeros((7, 40, 128), F32)
     load.wait()
 
     def residual(count, rebuilt):
@@ -183,7 +185,7 @@
 
     def iteration(number):
         first = number == 0
-        sem = 14 * number
+        sem = 12 * number
 
         def old(ref, *index):
             return 0.0 if first else ref[index]
@@ -206,139 +208,180 @@
 
         loop(8, time_rows)
 
+        qr, pr, cr = f0qr.at[number], f0pr.at[number], f0yr.at[number]
+        xr, yr = f1xr.at[number], f1yr.at[number]
         for tb in range(2):
-            f0x[tb] = q_of(t0[tb, 0:64, :], t0[tb, 72:136, :])
-            f0y[tb] = q_even(t0[tb, pl.ds(0, 32, stride=72), :], t0[tb, pl.ds(1, 32, stride=72), :])
-            f0c[tb : tb + 1, :] = q_even(f0x[tb, 0:1, :], f0x[tb, 1:2, :])
+            f0q[tb, 0:64, :] = q_of(t0[tb, 0:64, :], t0[tb, 72:136, :])
+            f0p[tb, 0:64, :] = p_of(t0[tb, 2160:2224, :], t0[tb, 2232:2296, :])
+            column = [t0[tb, pl.ds(y, 32, stride=72), :] for y in (0, 1, 62, 63)]
+            f0y[tb, 0:32, :] = q_even(column[0], column[1])
+            f0y[2 + tb, 0:32, :] = p_of(column[2], column[3])
+            for block, source in ((27, f0q), (36, f0p)):
+                f1y[tb, block : block + 1, :] = q_even(source[tb, 0:1, :], source[tb, 1:2, :])
+                f1y[3 + tb, block : block + 1, :] = p_of(source[tb, 62:63, :], source[tb, 63:64, :])
+        t0[0, pl.ds(64, 32, stride=72), :] = jnp.zeros((32, 128), F32)
+
+        def y_low(read):
+            e = [read(j) for j in range(4)]
+            return low_of(p_of(e[0], e[1]), q_of(e[2], e[3]))
+
+        def low_pair(k):
+            return [
+                [
+                    y_low(lambda j: t0[0, pl.ds((2 * k + i) * 72 + 16 * chunk + j, 8, stride=2), :])
+                    for i in range(2)
+                ]
+                for chunk in range(4)
+            ]
+
+        def low_store(k, chunk, value):
+            e1[pl.ds((k + 4) * 40 + 4 + 8 * chunk, 8), :] = value
+
+        def low_step(k, ps):
+            after = low_pair(k + 1)
+            for chunk in range(4):
+                low_store(k, chunk, low_of(ps[chunk], q_of(*after[chunk])))
+            return tuple(p_of(*one) for one in after)
+
+        ps = lax.fori_loop(0, 15, low_step, tuple(p_of(*one) for one in low_pair(0)), unroll=5)
+        for chunk in range(4):
+            low_store(15, chunk, ps[chunk])
+            low_store(19, chunk, y_low(lambda j: f0q[0, pl.ds(16 * chunk + j, 8, stride=2), :]))
+        e1[pl.ds(161, 16, stride=40), :] = ROOT_THREE * y_low(lambda j: f0y[0, pl.ds(j, 16, stride=2), :])
+        e1[921:922, :] = q_of(f0q[0, 0:1, :], f0q[0, 1:2, :])
+
+        for base, part in ((0, slice(4, 36)), (1, slice(1, 2))):
+
+            def entry(i):
+                return e1[i * 40 + part.start : i * 40 + part.stop, :]
+
+            values = functionals(lambda i: entry(4 + i), 16, entry(23), q_of)
+            for n, value in enumerate(values):
+                tile = 0 if n < 3 else 104
+                n = n if n < 3 else n - 3
+                start = tile + n if base else tile + 8 + 32 * n
+                f1x[start : start + (1 if base else 32), :] = value
+        for source, base, size, stride, level1_q, target in (
+            (e1, 164, 16, 40, pl.ds(161, 16, stride=40), 0),
+            (e1, 924, 1, 1, pl.ds(921, 1), 16),
+            (f1x, 8, 3, 32, pl.ds(0, 3), 24),
+            (f1x, 112, 4, 32, pl.ds(104, 4), 32),
+        ):
+
+            def entry(i):
+                return source[pl.ds(base + i, size, stride=stride) if size > 1 else pl.ds(base + i, 1), :]
+
+            for n, value in enumerate(functionals(entry, 32, source[level1_q, :], q_even)):
+                f1y[n, target : target + size, :] = value
         if first:
             pl.semaphore_wait(barrier, 8)
+        f1 = send(sem + 4, [
+            (f1x.at[0:104], xr.at[0:104], -1, 0),
+            (f1x.at[104:240], xr.at[104:240], 1, 0),
+            (f1y.at[0:3, 0:24], yr.at[0:3, 0:24], 0, -1),
+            (f1y.at[3:7, 0:24], yr.at[3:7, 0:24], 0, 1),
+            (f1y.at[0:3, 24:32], yr.at[0:3, 24:32], -1, -1),
+            (f1y.at[3:7, 24:32], yr.at[3:7, 24:32], -1, 1),
+            (f1y.at[0:3, 32:40], yr.at[0:3, 32:40], 1, -1),
+            (f1y.at[3:7, 32:40], yr.at[3:7, 32:40], 1, 1),
+        ])
+
         f0 = send(sem, [
-            (f0x, t0.at[:, 2304:2368, :], -1, 0),
-            (f0y, f0yr, 0, -1),
-            (f0c, f0cr, -1, -1),
+            (f0q.at[:, 0:64], qr.at[:, 0:64], -1, 0),
+            (f0p.at[:, 0:64], pr.at[:, 0:64], 1, 0),
+            (f0y.at[0:2], cr.at[0:2], 0, -1),
+            (f0y.at[2:4], cr.at[2:4], 0, 1),
         ])
 
-        def y_level1(row, chunk, tb):
-            e = [t0[tb, pl.ds(row * 72 + 16 * chunk + j, 8, stride=2), :] for j in range(4)]
+        def y_level1(read):
+            e = [read(j) for j in range(4)]
             p, q = p_of(e[0], e[1]), q_of(e[2], e[3])
             return [low_of(p, q), high_of(p, q)]
 
+        def y_own(row, chunk, tb):
+            return y_level1(lambda j: t0[tb, pl.ds(row * 72 + 16 * chunk + j, 8, stride=2), :])
+
+        def y_halo(ref, chunk, tb):
+            return y_level1(lambda j: ref[tb, pl.ds(16 * chunk + j, 8, stride=2), :])
+
         def level1_store(k, chunk, tb, yb, p, q):
             for xb in range(2):
-                value = high_of(p, q) if xb else low_of(p, q)
                 band = 4 * xb + 2 * yb + tb
-                if band == 0:
-                    e1[pl.ds((k + 4) * 40 + 4 + 8 * chunk, 8), :] = value
-                else:
+                if band:
+                    value = high_of(p, q) if xb else low_of(p, q)
                     place = rows((k + 1) * 40 + 8 + 8 * chunk, 8)
                     c1[band - 1, place, :] = shrink(old(c1, band - 1, place, slice(None)) + value)
 
-        def level1(chunks):
-            parts = [(chunk, tb) for chunk in chunks for tb in range(2)]
-
-            def pair(k):
-                result = []
-                for chunk, tb in parts:
-                    first_row = y_level1(2 * k, chunk, tb)
-                    second_row = y_level1(2 * k + 1, chunk, tb)
-                    for yb in range(2):
-                        result.append((first_row[yb], second_row[yb]))
-                return result
-
-            def step(i, ps):
-                k = i + 1
-                after = pair(k)
+        def pair(k, parts):
+            result = []
+            for chunk, tb in parts:
+                first_row, second_row = y_own(2 * k, chunk, tb), y_own(2 * k + 1, chunk, tb)
+                result += [(first_row[yb], second_row[yb]) for yb in range(2)]
+            return result
+
+        def store_all(k, parts, ps, qs):
+            for n, (chunk, tb) in enumerate(parts):
+                for yb in range(2):
+                    level1_store(k, chunk, tb, yb, ps[2 * n + yb], qs[2 * n + yb])
+
+        def level1(parts):
+            def step(k, ps):
+                after = pair(k + 1, parts)
+                store_all(k, parts, ps, [q_of(*one) for one in after])
+                return tuple(p_of(*one) for one in after)
+
+            return lax.fori_loop(0, 15, step, tuple(p_of(*one) for one in pair(0, parts)), unroll=3)
+
+        def level1_ends(parts, last):
+            before = [value for part in parts for value in y_halo(pr, *part)]
+            store_all(-1, parts, before, [q_of(*one) for one in pair(0, parts)])
+            store_all(15, parts, last, [value for part in parts for value in y_halo(qr, *part)])
+
+        inner = [(chunk, tb) for chunk in range(3) for tb in range(2)]
+        edge = [(3, tb) for tb in range(2)]
+        inner_last = level1(inner)
+
+        def time_up1_pieces(pieces):
+            for b in range(1, 4):
+                values = jnp.concatenate(
+                    [
+                        jnp.concatenate([c1[band, start:stop, :] for start, stop in pieces], axis=0)
+                        for band in (2 * b - 1, 2 * b)
+                    ],
+                    axis=1,
+                )
+                result = times(values, m1t)
                 n = 0
-                for chunk, tb in parts:
-                    for yb in range(2):
-                        level1_store(i, chunk, tb, yb, ps[n], q_of(*after[n]))
-                        n += 1
-                return tuple(p_of(*one) for one in after)
-
-            return lax.fori_loop(0, 15, step, tuple(p_of(*one) for one in pair(0)), unroll=3)
-
-        def level1_last(chunks, ps):
-            n = 0
-            for chunk in chunks:
-                for tb in range(2):
-                    halo_row = y_level1(32, chunk, tb)
-                    for yb in range(2):
-                        level1_store(15, chunk, tb, yb, ps[n], halo_row[yb])
-                        n += 1
-
-        inner = level1((0, 1, 2))
-        wait(f0)
-        for tb in range(2):
-            t0[tb, pl.ds(64, 32, stride=72), :] = f0yr[tb]
-            t0[tb, 2368:2369, :] = f0cr[tb : tb + 1, :]
-        level1_last((0, 1, 2), inner)
-        level1_last((3,), level1((3,)))
-
-        for n, value in enumerate(
-            functionals(lambda i: e1[(4 + i) * 40 + 4 : (4 + i) * 40 + 36, :], 16, q_of)
-        ):
-            f1x[n * 32 : (n + 1) * 32, :] = value
-        for start, size, stride, target, offset in ((164, 16, 40, 0, e1), (0, 2, 32, 16, f1x), (64, 4, 32, 24, f1x)):
-            for n, value in enumerate(
-                functionals(lambda i: offset[pl.ds(start + i, size, stride=stride), :], 32, q_even)
-            ):
-                f1y[n, target : target + size, :] = value
-        xr, yr = f1xr.at[number], f1yr.at[number]
-        f1 = send(sem + 3, [
-            (f1x.at[0:64], xr.at[0:64], -1, 0),
-            (f1x.at[64:192], xr.at[64:192], 1, 0),
-            (f1y.at[0:2, 0:16], yr.at[0:2, 0:16], 0, -1),
-            (f1y.at[2:6, 0:16], yr.at[2:6, 0:16], 0, 1),
-            (f1y.at[0:2, 16:24], yr.at[0:2, 16:24], -1, -1),
-            (f1y.at[2:6, 16:24], yr.at[2:6, 16:24], -1, 1),
-            (f1y.at[0:2, 24:32], yr.at[0:2, 24:32], 1, -1),
-            (f1y.at[2:6, 24:32], yr.at[2:6, 24:32], 1, 1),
-        ])
-
-        def i1_rows(read):
-            bands = [read(b) for b in range(7)]
-            return bands, [bands[3], bands[4] + RATIO * bands[0], bands[5] + RATIO * bands[1], bands[6] + RATIO * bands[2]]
-
-        _, values = i1_rows(lambda b: c1[b, 648:680, :])
-        for n in range(4):
-            i1x[n * 32 : (n + 1) * 32, :] = values[n]
-        bands, _ = i1_rows(lambda b: c1[b, pl.ds(79, 16, stride=40), :])
-        values = [bands[1], bands[2] + RATIO * bands[0], bands[5] + RATIO * bands[3], bands[6] + RATIO * bands[4]]
-        for n in range(4):
-            i1y[n * 16 : (n + 1) * 16, :] = values[n]
-        _, values = i1_rows(lambda b: c1[b, 679:680, :])
-        for n in range(2):
-            i1c[n : n + 1, :] = RATIO * values[n] + values[2 + n]
-        i1 = send(sem + 11, [(i1x, i1xr, 1, 0), (i1y, i1yr, 0, 1), (i1c, i1cr, 1, 1)])
-
-        def time_up1_own(n):
-            place = rows(40 + n * 128, 128)
-            for b in range(1, 4):
-                values = jnp.concatenate([c1[2 * b - 1, place, :], c1[2 * b, place, :]], axis=1)
-                result = times(values, m1t)
-                s1[0, b, place, :] = result[:, :128]
-                s1[1, b, place, :] = result[:, 128:]
-
-        loop(5, time_up1_own, unroll=5)
+                for start, stop in pieces:
+                    for th in range(2):
+                        s1[th, b, start:stop, :] = result[n : n + stop - start, th * 128 : (th + 1) * 128]
+                    n += stop - start
+
+        time_up1_pieces([(row * 40 + 8, row * 40 + 32) for row in range(1, 16)])
         wait(f1)
-        e1[804:836, :] = xr[0:32, :]
-        e1[844:876, :] = xr[32:64, :]
-        for n in range(4):
-            e1[n * 40 + 4 : n * 40 + 36, :] = xr[64 + n * 32 : 96 + n * 32, :]
+
+        for tile, first_row, count in ((0, 20, 3), (104, 0, 4)):
+            e1[pl.ds(first_row * 40 + 1, count, stride=40), :] = xr[tile : tile + count, :]
+            for n in range(count):
+                row = (first_row + n) * 40
+                e1[row + 4 : row + 36, :] = xr[tile + 8 + 32 * n : tile + 40 + 32 * n, :]
         for n, place in enumerate(PLACES):
             e1[pl.ds(160 + place, 16, stride=40), :] = yr[n, 0:16, :]
-            e1[pl.ds(800 + place, 2, stride=40), :] = yr[n, 16:18, :]
-            e1[pl.ds(place, 4, stride=40), :] = yr[n, 24:28, :]
+            e1[pl.ds(920 + place, 1), :] = yr[n, 16:17, :]
+            e1[pl.ds(800 + place, 3, stride=40), :] = yr[n, 24:27, :]
+            e1[pl.ds(place, 4, stride=40), :] = yr[n, 32:36, :]
+        for target, source in ((19, 22), (2, 23)):
+            e1[target * 40 : (target + 1) * 40, :] += RATIO * e1[source * 40 : (source + 1) * 40, :]
+        for target, source in ((35, 37), (3, 1)):
+            place = pl.ds(target, 22, stride=40)
+            e1[place, :] = e1[place, :] + RATIO * e1[pl.ds(source, 22, stride=40), :]
+        for place in (1, 37):
+            e1[pl.ds(place, 22, stride=40), :] = jnp.zeros((22, 128), F32)
 
         def time_level2(n):
             t2[rows(n * 176, 176), :] = times(e1[rows(n * 176, 176), :], m2)
 
         loop(5, time_level2, unroll=5)
-
-        def pairs(row, before, first_pair, count, last):
-            ps = [row(before), p_of(row(first_pair), row(first_pair + 1))]
-            qs = [q_of(row(first_pair), row(first_pair + 1))]
-            return ps, qs
 
         def t2_row(i):
             return t2[i * 40 : (i + 1) * 40, :]
@@ -464,21 +507,32 @@
 
         loop(18, y_up2, unroll=6)
 
-        wait(i1)
+        wait(f0)
         for tb in range(2):
-            halo[tb, 0:32, :] = i1xr[tb * 32 : (tb + 1) * 32, :]
-            halo[tb, 32:64, :] = i1xr[(2 + tb) * 32 : (3 + tb) * 32, :]
-            halo[tb, 64:80, :] = i1yr[tb * 16 : (tb + 1) * 16, :]
-            halo[tb, 80:96, :] = i1yr[(2 + tb) * 16 : (3 + tb) * 16, :]
-            halo[tb, 96:97, :] = i1cr[tb : tb + 1, :]
-        result = times(jnp.concatenate([halo[0], halo[1]], axis=1), m1t)
-        for th in range(2):
-            part = result[:, th * 128 : (th + 1) * 128]
-            s1[th, 2, 8:40, :] = part[0:32]
-            s1[th, 3, 8:40, :] = part[32:64]
-            s1[th, 1, pl.ds(47, 16, stride=40), :] = part[64:80]
-            s1[th, 3, pl.ds(47, 16, stride=40), :] = part[80:96]
-            s1[th, 3, 7:8, :] = part[96:97]
+            t0[tb, pl.ds(64, 32, stride=72), :] = cr[tb, 0:32, :]
+            qr[tb, 64:65, :] = yr[tb, 27:28, :]
+            pr[tb, 64:65, :] = yr[tb, 36:37, :]
+            for place, p, q, scale in (
+                (pl.ds(2, 32), cr[2 + tb, 0:32, :], ROOT_THREE * f0y[tb, 0:32, :], 1.0),
+                (pl.ds(0, 1), yr[3 + tb, 36:37, :], q_of(pr[tb, 0:1, :], pr[tb, 1:2, :]), 1.0),
+                (pl.ds(34, 1), yr[3 + tb, 27:28, :], q_of(qr[tb, 0:1, :], qr[tb, 1:2, :]), 1.0 / ROOT_THREE),
+            ):
+                cb[tb, place, :] = scale * low_of(p, q)
+                cb[2 + tb, place, :] = scale * high_of(p, q)
+        level1_ends(inner, inner_last)
+        level1_ends(edge, level1(edge))
+        for yb in range(2):
+            for tb in range(2):
+                e = [cb[2 * yb + tb, pl.ds(j, 17, stride=2), :] for j in range(4)]
+                p, q = p_of(e[0], e[1]), q_of(e[2], e[3])
+                for xb in range(2):
+                    band = 4 * xb + 2 * yb + tb
+                    if band:
+                        value = high_of(p, q) if xb else low_of(p, q)
+                        place = pl.ds(7, 17, stride=40)
+                        c1[band - 1, place, :] = shrink(old(c1, band - 1, place, slice(None)) + value)
+
+        time_up1_pieces([(0, 40), (640, 680)] + [(row * 40 + y, row * 40 + y + 8) for row in range(1, 16) for y in (0, 32)])
 
         def time_up1(n):
             place = rows(n * 136, 136)
@@ -542,16 +596,15 @@
     scratch = [
         pltpu.VMEM((32, 64, 256), jnp.int32),
         b(768, 256), b(768, 256), b(384, 128), b(384, 128), b(384, 128), b(384, 128),
-        v(2, 33 * 72, 128), v(7, 17 * 40, 128), v(22 * 40, 128),
+        v(2, 32 * 72, 128), v(7, 17 * 40, 128), v(24 * 40, 128),
         v(22 * 40, 128), v(2, 12 * 40, 128), v(4, 10 * 24, 128), v(12 * 24, 128),
         v(12 * 24, 128), v(2, 6 * 24, 128), v(4, 6 * 16, 128),
         v(4, 6 * 16, 128), v(2, 10 * 16, 128), v(10 * 24, 128),
         v(4, 10 * 24, 128), v(2, 18 * 24, 128), v(18 * 40, 128),
-        v(2, 4, 17 * 40, 128), v(2, 32 * 64, 128), v(2, 104, 128),
-        v(2, 64, 128), v(2, 32, 128), v(8, 128), v(2, 32, 128), v(8, 128),
-        v(192, 128), v(6, 32, 128), v(2, 192, 128), v(2, 6, 32, 128),
-        v(128, 128), v(64, 128), v(8, 128), v(128, 128), v(64, 128), v(8, 128),
-        pltpu.SemaphoreType.DMA((1,)), pltpu.SemaphoreType.DMA((28,)), pltpu.SemaphoreType.DMA((28,)),
+        v(2, 4, 17 * 40, 128), v(2, 32 * 64, 128), v(4, 40, 128),
+        v(2, 72, 128), v(2, 72, 128), v(4, 40, 128), v(2, 2, 72, 128), v(2, 2, 72, 128), v(2, 4, 40, 128),
+        v(240, 128), v(7, 40, 128), v(2, 240, 128), v(2, 7, 40, 128),
+        pltpu.SemaphoreType.DMA((1,)), pltpu.SemaphoreType.DMA((24,)), pltpu.SemaphoreType.DMA((24,)),
     ]
 
     def on_device(counts):

time: 37.2 us -> 31.1 us (0.84)
  Pallas kernels: 35.7 us -> 29.7 us
    pallas_call x1, Pallas kernels: 35.7 us -> 29.7 us  [on_device(): pl.pallas_call(functools.partial(kernel, nx, ny), out_shape=jax.ShapeDtyp...]
where the time goes in v2:
time: 31.1 us; the launch traced here: 31 us
  Pallas kernels  29.7 us (95%)
  local copies, waits for them, and re-layouts  1.32 us (4%)
    pallas_call x1, Pallas kernels, on_device(): pl.pallas_call(functools.partial(kernel, nx, ny), out_shape=jax.ShapeDtyp...  29.7 us
    unnamed x1, local copies, waits for them, and re-layouts  1.32 us

profile of v2, /device:TPU:0, one launch (start us, length us, event | category | flops | bytes accessed | tf_op | source)
XLA Modules:
  0.0 31.0 jit_solution(4678497563587229198)
XLA Ops:
  0.0 29.7 %shard_map.17 = f32[32,64,256]{2,1,0:T(8,128)S(1)} custom-call(s32[32,64,256]{2,1,0:T(8,128)} %counts_hbm.1), custom_call_target="tpu_custom_call" | custom-call | tf_op jit(solution)/shard_map/pallas_call | solution.py:611
  29.7 1.3 %copy.3 = f32[32,64,256]{2,1,0:T(8,128)} copy(f32[32,64,256]{2,1,0:T(8,128)S(1)} %shard_map.17) | data formatting | bytes 4194304

commit v3 on v2

--- a/solution.py
+++ b/solution.py
@@ -25,6 +25,7 @@
 BF16 = jnp.bfloat16
 
 PLACES = [36, 39, 37, 0, 2, 3, 38]
+CORNERS = [((-1, -1), 9), ((-1, 1), 12), ((1, -1), 12), ((1, 1), 16)]
 
 
 def shrink(values):
@@ -109,8 +110,8 @@
     counts_hbm, out, counts, m1, m1t, m2, m2t, m3, m3t,
     t0, c1, e1, t2, a2, c2, e2, t3, a3, c3,
     s3, p3, d2, s2, p2, d1, s1, reb, cb,
-    f0q, f0p, f0y, f0qr, f0pr, f0yr,
-    f1x, f1y, f1xr, f1yr,
+    f0q, f0p, fq, fp, f0y, f0qr, f0pr, f0yr,
+    f1x, f1y, f1xr, f1yr, fc, fcr,
     local_sem, send_sem, recv_sem,
 ):
     gx = lax.axis_index("gx")
@@ -152,18 +153,9 @@
             copy.wait()
 
     build_matrix(m1, 256, 256, False)
-    build_matrix(m1t, 256, 256, True)
-    build_matrix(m2, 128, 128, False)
-    build_matrix(m2t, 128, 128, True)
-    build_matrix(m3, 64, 128, False)
-    build_matrix(m3t, 64, 128, True)
     for ref in (f0q, f0p):
         for tb in range(2):
             ref[tb, 64:72, :] = jnp.zeros((8, 128), F32)
-    for ref in (f0qr, f0pr):
-        for number in range(2):
-            for tb in range(2):
-                ref[number, tb, 64:72, :] = jnp.zeros((8, 128), F32)
     for n in range(4):
         f0y[n, 32:40, :] = jnp.zeros((8, 128), F32)
         for place in (1, 35):
@@ -173,7 +165,7 @@
     for place in (1, 21):
         e2[pl.ds(place, 12, stride=24), :] = jnp.zeros((12, 128), F32)
     e1[...] = jnp.zeros((960, 128), F32)
-    f1y[...] = jnp.zeros((7, 40, 128), F32)
+    f1y[...] = jnp.zeros((7, 24, 128), F32)
     load.wait()
 
     def residual(count, rebuilt):
@@ -183,12 +175,15 @@
             return weight * observed
         return weight * (observed - rebuilt)
 
-    def iteration(number):
+    def iteration(number, synthesis):
         first = number == 0
         sem = 12 * number
 
         def old(ref, *index):
             return 0.0 if first else ref[index]
+
+        qr, pr, cr = f0qr.at[number], f0pr.at[number], f0yr.at[number]
+        xr, yr = f1xr.at[number], f1yr.at[number]
 
         def time_rows(n):
             count = counts[pl.ds(n * 4, 4)].reshape(256, 256)
@@ -206,19 +201,6 @@
                         i * 64 : (i + 1) * 64, tb * 128 : (tb + 1) * 128
                     ]
 
-        loop(8, time_rows)
-
-        qr, pr, cr = f0qr.at[number], f0pr.at[number], f0yr.at[number]
-        xr, yr = f1xr.at[number], f1yr.at[number]
-        for tb in range(2):
-            f0q[tb, 0:64, :] = q_of(t0[tb, 0:64, :], t0[tb, 72:136, :])
-            f0p[tb, 0:64, :] = p_of(t0[tb, 2160:2224, :], t0[tb, 2232:2296, :])
-            column = [t0[tb, pl.ds(y, 32, stride=72), :] for y in (0, 1, 62, 63)]
-            f0y[tb, 0:32, :] = q_even(column[0], column[1])
-            f0y[2 + tb, 0:32, :] = p_of(column[2], column[3])
-            for block, source in ((27, f0q), (36, f0p)):
-                f1y[tb, block : block + 1, :] = q_even(source[tb, 0:1, :], source[tb, 1:2, :])
-                f1y[3 + tb, block : block + 1, :] = p_of(source[tb, 62:63, :], source[tb, 63:64, :])
         t0[0, pl.ds(64, 32, stride=72), :] = jnp.zeros((32, 128), F32)
 
         def y_low(read):
@@ -237,72 +219,131 @@
         def low_store(k, chunk, value):
             e1[pl.ds((k + 4) * 40 + 4 + 8 * chunk, 8), :] = value
 
-        def low_step(k, ps):
-            after = low_pair(k + 1)
-            for chunk in range(4):
-                low_store(k, chunk, low_of(ps[chunk], q_of(*after[chunk])))
-            return tuple(p_of(*one) for one in after)
-
-        ps = lax.fori_loop(0, 15, low_step, tuple(p_of(*one) for one in low_pair(0)), unroll=5)
+        def low_band(first_k, count):
+            def low_step(n, ps):
+                k = first_k + n
+                after = low_pair(k + 1)
+                for chunk in range(4):
+                    low_store(k, chunk, low_of(ps[chunk], q_of(*after[chunk])))
+                return tuple(p_of(*one) for one in after)
+
+            ps = tuple(p_of(*one) for one in low_pair(first_k))
+            return lax.fori_loop(0, count, low_step, ps, unroll=4)
+
+        def y_level1_q(places):
+            e1[pl.ds(161 + 40 * places, 8, stride=40), :] = ROOT_THREE * y_low(
+                lambda j: f0y[0, pl.ds(2 * places + j, 8, stride=2), :]
+            )
+
+        def x_functionals(kind):
+            for base, part in ((0, slice(4, 36)), (1, slice(1, 2))):
+
+                def entry(i):
+                    return e1[i * 40 + part.start : i * 40 + part.stop, :]
+
+                values = functionals(lambda i: entry(4 + i), 16, entry(23), q_of)
+                for n, value in enumerate(values[3:] if kind else values[:3]):
+                    tile = 104 * kind
+                    start = tile + n if base else tile + 8 + 32 * n
+                    f1x[start : start + (1 if base else 32), :] = value
+
+        def half(number_of_half):
+            if synthesis is not None:
+                synthesis(8 * number_of_half)
+            loop(4, lambda n: time_rows(n + 4 * number_of_half))
+            start = 16 * number_of_half * 72
+            for tb in range(2):
+                column = [t0[tb, pl.ds(start + y, 16, stride=72), :] for y in (0, 1, 62, 63)]
+                place = pl.ds(16 * number_of_half, 16)
+                f0y[tb, place, :] = q_even(column[0], column[1])
+                f0y[2 + tb, place, :] = p_of(column[2], column[3])
+                if number_of_half:
+                    f0p[tb, 0:64, :] = p_of(t0[tb, 2160:2224, :], t0[tb, 2232:2296, :])
+                else:
+                    f0q[tb, 0:64, :] = q_of(t0[tb, 0:64, :], t0[tb, 72:136, :])
+
+        half(1)
+        ps = low_band(8, 7)
         for chunk in range(4):
             low_store(15, chunk, ps[chunk])
+        y_level1_q(8)
+        x_functionals(1)
+        x_after = [(f1x.at[104:240], xr.at[104:240], 1, 0)]
+        if not first:
+            f1 = send(sem + 4, x_after)
+
+        half(0)
+        low_band(0, 8)
+        for chunk in range(4):
             low_store(19, chunk, y_low(lambda j: f0q[0, pl.ds(16 * chunk + j, 8, stride=2), :]))
-        e1[pl.ds(161, 16, stride=40), :] = ROOT_THREE * y_low(lambda j: f0y[0, pl.ds(j, 16, stride=2), :])
+        y_level1_q(0)
         e1[921:922, :] = q_of(f0q[0, 0:1, :], f0q[0, 1:2, :])
-
-        for base, part in ((0, slice(4, 36)), (1, slice(1, 2))):
-
-            def entry(i):
-                return e1[i * 40 + part.start : i * 40 + part.stop, :]
-
-            values = functionals(lambda i: entry(4 + i), 16, entry(23), q_of)
-            for n, value in enumerate(values):
-                tile = 0 if n < 3 else 104
-                n = n if n < 3 else n - 3
-                start = tile + n if base else tile + 8 + 32 * n
-                f1x[start : start + (1 if base else 32), :] = value
+        x_functionals(0)
+
+        for tb in range(2):
+            for n, source in ((0, f0q), (2, f0p)):
+                place = slice(CORNERS[n][1] + tb, CORNERS[n][1] + tb + 1)
+                fc[n, place, :] = q_even(source[tb, 0:1, :], source[tb, 1:2, :])
+                place = slice(CORNERS[n + 1][1] + tb, CORNERS[n + 1][1] + tb + 1)
+                fc[n + 1, place, :] = p_of(source[tb, 62:63, :], source[tb, 63:64, :])
         for source, base, size, stride, level1_q, target in (
             (e1, 164, 16, 40, pl.ds(161, 16, stride=40), 0),
             (e1, 924, 1, 1, pl.ds(921, 1), 16),
-            (f1x, 8, 3, 32, pl.ds(0, 3), 24),
-            (f1x, 112, 4, 32, pl.ds(104, 4), 32),
+            (f1x, 8, 3, 32, pl.ds(0, 3), None),
+            (f1x, 112, 4, 32, pl.ds(104, 4), None),
         ):
 
             def entry(i):
                 return source[pl.ds(base + i, size, stride=stride) if size > 1 else pl.ds(base + i, 1), :]
 
             for n, value in enumerate(functionals(entry, 32, source[level1_q, :], q_even)):
-                f1y[n, target : target + size, :] = value
+                if target is None:
+                    corner, start = 2 * (size - 3) + (n > 2), (n - 3 * (n > 2)) * size
+                    fc[corner, start : start + size, :] = value
+                else:
+                    f1y[n, target : target + size, :] = value
         if first:
             pl.semaphore_wait(barrier, 8)
-        f1 = send(sem + 4, [
+        f1 = ([] if first else f1) + send(sem + 5, [
+            (fc.at[n, 0 : used + 2], fcr.at[number, n, 0 : used + 2], dx, dy)
+            for n, ((dx, dy), used) in enumerate(CORNERS)
+        ] + [
             (f1x.at[0:104], xr.at[0:104], -1, 0),
-            (f1x.at[104:240], xr.at[104:240], 1, 0),
-            (f1y.at[0:3, 0:24], yr.at[0:3, 0:24], 0, -1),
-            (f1y.at[3:7, 0:24], yr.at[3:7, 0:24], 0, 1),
-            (f1y.at[0:3, 24:32], yr.at[0:3, 24:32], -1, -1),
-            (f1y.at[3:7, 24:32], yr.at[3:7, 24:32], -1, 1),
-            (f1y.at[0:3, 32:40], yr.at[0:3, 32:40], 1, -1),
-            (f1y.at[3:7, 32:40], yr.at[3:7, 32:40], 1, 1),
+            (f1y.at[0:3], yr.at[0:3], 0, -1),
+            (f1y.at[3:7], yr.at[3:7], 0, 1),
         ])
-
-        f0 = send(sem, [
-            (f0q.at[:, 0:64], qr.at[:, 0:64], -1, 0),
-            (f0p.at[:, 0:64], pr.at[:, 0:64], 1, 0),
-            (f0y.at[0:2], cr.at[0:2], 0, -1),
-            (f0y.at[2:4], cr.at[2:4], 0, 1),
-        ])
+        if first:
+            f1 += send(sem + 4, x_after)
 
         def y_level1(read):
             e = [read(j) for j in range(4)]
             p, q = p_of(e[0], e[1]), q_of(e[2], e[3])
             return [low_of(p, q), high_of(p, q)]
 
+        def y_halo(ref, chunk, tb):
+            return y_level1(lambda j: ref[tb, pl.ds(16 * chunk + j, 8, stride=2), :])
+
+        for source, target in ((f0q, fq), (f0p, fp)):
+            for chunk in range(4):
+                for n, value in enumerate(y_halo(source, chunk, 1) + y_halo(source, chunk, 0)[1:]):
+                    target[32 * n + 8 * chunk : 32 * n + 8 * chunk + 8, :] = value
+            target[96:97, :] = q_of(source[1, 0:1, :], source[1, 1:2, :])
+        f0 = send(sem, [
+            (fq.at[0:97], qr.at[0:97], -1, 0),
+            (fp.at[0:97], pr.at[0:97], 1, 0),
+            (f0y.at[0:2], cr.at[0:2], 0, -1),
+            (f0y.at[2:4], cr.at[2:4], 0, 1),
+        ])
+
+        if first:
+            build_matrix(m1t, 256, 256, True)
+            build_matrix(m2, 128, 128, False)
+            build_matrix(m2t, 128, 128, True)
+            build_matrix(m3, 64, 128, False)
+            build_matrix(m3t, 64, 128, True)
+
         def y_own(row, chunk, tb):
             return y_level1(lambda j: t0[tb, pl.ds(row * 72 + 16 * chunk + j, 8, stride=2), :])
-
-        def y_halo(ref, chunk, tb):
-            return y_level1(lambda j: ref[tb, pl.ds(16 * chunk + j, 8, stride=2), :])
 
         def level1_store(k, chunk, tb, yb, p, q):
             for xb in range(2):
@@ -332,10 +373,16 @@
 
             return lax.fori_loop(0, 15, step, tuple(p_of(*one) for one in pair(0, parts)), unroll=3)
 
+        def received(ref, low_row, chunk, tb):
+            if tb:
+                return [ref[32 * yb + 8 * chunk : 32 * yb + 8 * chunk + 8, :] for yb in range(2)]
+            place = low_row + 8 * chunk
+            return [xr[place : place + 8, :], ref[64 + 8 * chunk : 72 + 8 * chunk, :]]
+
         def level1_ends(parts, last):
-            before = [value for part in parts for value in y_halo(pr, *part)]
+            before = [value for part in parts for value in received(pr, 176, *part)]
             store_all(-1, parts, before, [q_of(*one) for one in pair(0, parts)])
-            store_all(15, parts, last, [value for part in parts for value in y_halo(qr, *part)])
+            store_all(15, parts, last, [value for part in parts for value in received(qr, 72, *part)])
 
         inner = [(chunk, tb) for chunk in range(3) for tb in range(2)]
         edge = [(3, tb) for tb in range(2)]
@@ -368,8 +415,9 @@
         for n, place in enumerate(PLACES):
             e1[pl.ds(160 + place, 16, stride=40), :] = yr[n, 0:16, :]
             e1[pl.ds(920 + place, 1), :] = yr[n, 16:17, :]
-            e1[pl.ds(800 + place, 3, stride=40), :] = yr[n, 24:27, :]
-            e1[pl.ds(place, 4, stride=40), :] = yr[n, 32:36, :]
+            corner, m = (1, n - 3) if n > 2 else (0, n)
+            e1[pl.ds(800 + place, 3, stride=40), :] = fcr[number, corner, 3 * m : 3 * m + 3, :]
+            e1[pl.ds(place, 4, stride=40), :] = fcr[number, corner + 2, 4 * m : 4 * m + 4, :]
         for target, source in ((19, 22), (2, 23)):
             e1[target * 40 : (target + 1) * 40, :] += RATIO * e1[source * 40 : (source + 1) * 40, :]
         for target, source in ((35, 37), (3, 1)):
@@ -510,12 +558,18 @@
         wait(f0)
         for tb in range(2):
             t0[tb, pl.ds(64, 32, stride=72), :] = cr[tb, 0:32, :]
-            qr[tb, 64:65, :] = yr[tb, 27:28, :]
-            pr[tb, 64:65, :] = yr[tb, 36:37, :]
+            corners = [fcr[number, n, used + tb : used + tb + 1, :] for n, (_, used) in enumerate(CORNERS)]
+            starts = []
+            for ref, low_row, corner in ((qr, 72, corners[0]), (pr, 176, corners[2])):
+                after = ROOT_THREE * corner
+                low, place, high = (ref, 31, 63) if tb else (xr, low_row + 31, 95)
+                low[place : place + 1, :] = low[place : place + 1, :] + RATIO * after
+                ref[high : high + 1, :] = ref[high : high + 1, :] + after
+                starts.append(ref[96:97, :] if tb else xr[low_row - 70 : low_row - 69, :])
             for place, p, q, scale in (
                 (pl.ds(2, 32), cr[2 + tb, 0:32, :], ROOT_THREE * f0y[tb, 0:32, :], 1.0),
-                (pl.ds(0, 1), yr[3 + tb, 36:37, :], q_of(pr[tb, 0:1, :], pr[tb, 1:2, :]), 1.0),
-                (pl.ds(34, 1), yr[3 + tb, 27:28, :], q_of(qr[tb, 0:1, :], qr[tb, 1:2, :]), 1.0 / ROOT_THREE),
+                (pl.ds(0, 1), corners[3], starts[1], 1.0),
+                (pl.ds(34, 1), corners[1], starts[0], 1.0 / ROOT_THREE),
             ):
                 cb[tb, place, :] = scale * low_of(p, q)
                 cb[2 + tb, place, :] = scale * high_of(p, q)
@@ -558,7 +612,8 @@
         def q_next(low, high):
             return high + RATIO * low
 
-        def up1(k, qs):
+        def up1(first_k, i, qs):
+            k = first_k + i
             after = []
             n = 0
             for chunk, th in up_parts:
@@ -571,11 +626,15 @@
                     n += 1
             return tuple(after)
 
-        start = tuple(q_next(*one) for chunk, th in up_parts for one in y_up1(0, chunk, th))
-        lax.fori_loop(0, 16, up1, start, unroll=2)
-
-    iteration(0)
-    iteration(1)
+        def synthesis_half(first_k):
+            start = tuple(q_next(*one) for chunk, th in up_parts for one in y_up1(first_k, chunk, th))
+            lax.fori_loop(0, 8, functools.partial(up1, first_k), start, unroll=2)
+
+        return synthesis_half
+
+    synthesis = iteration(1, iteration(0, None))
+    synthesis(0)
+    synthesis(8)
 
     def finish(r):
         for th in range(2):
@@ -602,8 +661,8 @@
         v(4, 6 * 16, 128), v(2, 10 * 16, 128), v(10 * 24, 128),
         v(4, 10 * 24, 128), v(2, 18 * 24, 128), v(18 * 40, 128),
         v(2, 4, 17 * 40, 128), v(2, 32 * 64, 128), v(4, 40, 128),
-        v(2, 72, 128), v(2, 72, 128), v(4, 40, 128), v(2, 2, 72, 128), v(2, 2, 72, 128), v(2, 4, 40, 128),
-        v(240, 128), v(7, 40, 128), v(2, 240, 128), v(2, 7, 40, 128),
+        v(2, 72, 128), v(2, 72, 128), v(104, 128), v(104, 128), v(4, 40, 128), v(2, 104, 128), v(2, 104, 128), v(2, 4, 40, 128),
+        v(240, 128), v(7, 24, 128), v(2, 240, 128), v(2, 7, 24, 128), v(4, 24, 128), v(2, 4, 24, 128),
         pltpu.SemaphoreType.DMA((1,)), pltpu.SemaphoreType.DMA((24,)), pltpu.SemaphoreType.DMA((24,)),
     ]
 

time: 31.1 us -> 27.7 us (0.89)
  Pallas kernels: 29.7 us -> 26.2 us
    pallas_call x1, Pallas kernels: 29.7 us -> 26.2 us  [on_device(): pl.pallas_call(functools.partial(kernel, nx, ny), out_shape=jax.ShapeDtyp...]
where the time goes in v3:
time: 27.7 us; the launch traced here: 27.5 us
  Pallas kernels  26.2 us (95%)
  local copies, waits for them, and re-layouts  1.32 us (5%)
    pallas_call x1, Pallas kernels, on_device(): pl.pallas_call(functools.partial(kernel, nx, ny), out_shape=jax.ShapeDtyp...  26.2 us
    unnamed x1, local copies, waits for them, and re-layouts  1.32 us

profile of v3, /device:TPU:0, one launch (start us, length us, event | category | flops | bytes accessed | tf_op | source)
XLA Modules:
  0.0 27.5 jit_solution(14830052762801158300)
XLA Ops:
  0.0 26.2 %shard_map.17 = f32[32,64,256]{2,1,0:T(8,128)S(1)} custom-call(s32[32,64,256]{2,1,0:T(8,128)} %counts_hbm.1), custom_call_target="tpu_custom_call" | custom-call | tf_op jit(solution)/shard_map/pallas_call | solution.py:670
  26.2 1.3 %copy.3 = f32[32,64,256]{2,1,0:T(8,128)} copy(f32[32,64,256]{2,1,0:T(8,128)S(1)} %shard_map.17) | data formatting | bytes 4194304

commit v4 on v3

--- a/solution.py
+++ b/solution.py
@@ -107,7 +107,7 @@
 
 def kernel(
     nx, ny,
-    counts_hbm, out, counts, m1, m1t, m2, m2t, m3, m3t,
+    counts_hbm, out, counts, weights, weighted, m1, m1t, m2, m2t, m3, m3t,
     t0, c1, e1, t2, a2, c2, e2, t3, a3, c3,
     s3, p3, d2, s2, p2, d1, s1, reb, cb,
     f0q, f0p, fq, fp, f0y, f0qr, f0pr, f0yr,
@@ -168,14 +168,7 @@
     f1y[...] = jnp.zeros((7, 24, 128), F32)
     load.wait()
 
-    def residual(count, rebuilt):
-        observed = count.astype(F32) * (1.0 / 64.0)
-        weight = 1.0 / (1.0 + jnp.abs(observed))
-        if rebuilt is None:
-            return weight * observed
-        return weight * (observed - rebuilt)
-
-    def iteration(number, synthesis):
+    def iteration(number):
         first = number == 0
         sem = 12 * number
 
@@ -186,14 +179,16 @@
         xr, yr = f1xr.at[number], f1yr.at[number]
 
         def time_rows(n):
-            count = counts[pl.ds(n * 4, 4)].reshape(256, 256)
+            place = rows(n * 256, 256)
             if first:
-                values = residual(count, None)
+                observed = counts[pl.ds(n * 4, 4)].reshape(256, 256).astype(F32) * (1.0 / 64.0)
+                weight = 1.0 / (1.0 + jnp.abs(observed))
+                values = weight * observed
+                weights[place, :] = weight
+                weighted[place, :] = values
             else:
-                rebuilt = jnp.concatenate(
-                    [reb[0, rows(n * 256, 256), :], reb[1, rows(n * 256, 256), :]], axis=1
-                )
-                values = residual(count, rebuilt)
+                rebuilt = jnp.concatenate([reb[0, place, :], reb[1, place, :]], axis=1)
+                values = weighted[place, :] - weights[place, :] * rebuilt
             result = times(values, m1)
             for i in range(4):
                 for tb in range(2):
@@ -248,8 +243,6 @@
                     f1x[start : start + (1 if base else 32), :] = value
 
         def half(number_of_half):
-            if synthesis is not None:
-                synthesis(8 * number_of_half)
             loop(4, lambda n: time_rows(n + 4 * number_of_half))
             start = 16 * number_of_half * 72
             for tb in range(2):
@@ -262,15 +255,40 @@
                 else:
                     f0q[tb, 0:64, :] = q_of(t0[tb, 0:64, :], t0[tb, 72:136, :])
 
+        def y_functionals(source, base, size, stride, level1_q, target):
+            def entry(i):
+                return source[pl.ds(base + i, size, stride=stride) if size > 1 else pl.ds(base + i, 1), :]
+
+            for n, value in enumerate(functionals(entry, 32, source[level1_q, :], q_even)):
+                if target is None:
+                    corner, start = 2 * (size - 3) + (n > 2), (n - 3 * (n > 2)) * size
+                    fc[corner, start : start + size, :] = value
+                else:
+                    f1y[n, target : target + size, :] = value
+
+        def corner_level1(n, source):
+            for tb in range(2):
+                place = slice(CORNERS[n][1] + tb, CORNERS[n][1] + tb + 1)
+                fc[n, place, :] = q_even(source[tb, 0:1, :], source[tb, 1:2, :])
+                place = slice(CORNERS[n + 1][1] + tb, CORNERS[n + 1][1] + tb + 1)
+                fc[n + 1, place, :] = p_of(source[tb, 62:63, :], source[tb, 63:64, :])
+
+        def corner_transfers(start):
+            return [
+                (fc.at[n, 0 : used + 2], fcr.at[number, n, 0 : used + 2], dx, dy)
+                for n, ((dx, dy), used) in enumerate(CORNERS)
+            ][start : start + 2]
+
         half(1)
         ps = low_band(8, 7)
         for chunk in range(4):
             low_store(15, chunk, ps[chunk])
         y_level1_q(8)
         x_functionals(1)
-        x_after = [(f1x.at[104:240], xr.at[104:240], 1, 0)]
-        if not first:
-            f1 = send(sem + 4, x_after)
+        y_functionals(f1x, 112, 4, 32, pl.ds(104, 4), None)
+        corner_level1(2, f0p)
+        after_transfers = corner_transfers(2) + [(f1x.at[104:240], xr.at[104:240], 1, 0)]
+        f1 = [] if first else send(sem + 4, after_transfers)
 
         half(0)
         low_band(0, 8)
@@ -279,41 +297,19 @@
         y_level1_q(0)
         e1[921:922, :] = q_of(f0q[0, 0:1, :], f0q[0, 1:2, :])
         x_functionals(0)
-
-        for tb in range(2):
-            for n, source in ((0, f0q), (2, f0p)):
-                place = slice(CORNERS[n][1] + tb, CORNERS[n][1] + tb + 1)
-                fc[n, place, :] = q_even(source[tb, 0:1, :], source[tb, 1:2, :])
-                place = slice(CORNERS[n + 1][1] + tb, CORNERS[n + 1][1] + tb + 1)
-                fc[n + 1, place, :] = p_of(source[tb, 62:63, :], source[tb, 63:64, :])
-        for source, base, size, stride, level1_q, target in (
-            (e1, 164, 16, 40, pl.ds(161, 16, stride=40), 0),
-            (e1, 924, 1, 1, pl.ds(921, 1), 16),
-            (f1x, 8, 3, 32, pl.ds(0, 3), None),
-            (f1x, 112, 4, 32, pl.ds(104, 4), None),
-        ):
-
-            def entry(i):
-                return source[pl.ds(base + i, size, stride=stride) if size > 1 else pl.ds(base + i, 1), :]
-
-            for n, value in enumerate(functionals(entry, 32, source[level1_q, :], q_even)):
-                if target is None:
-                    corner, start = 2 * (size - 3) + (n > 2), (n - 3 * (n > 2)) * size
-                    fc[corner, start : start + size, :] = value
-                else:
-                    f1y[n, target : target + size, :] = value
+        y_functionals(f1x, 8, 3, 32, pl.ds(0, 3), None)
+        corner_level1(0, f0q)
         if first:
             pl.semaphore_wait(barrier, 8)
-        f1 = ([] if first else f1) + send(sem + 5, [
-            (fc.at[n, 0 : used + 2], fcr.at[number, n, 0 : used + 2], dx, dy)
-            for n, ((dx, dy), used) in enumerate(CORNERS)
-        ] + [
-            (f1x.at[0:104], xr.at[0:104], -1, 0),
+            f1 = send(sem + 4, after_transfers)
+        f1 = f1 + send(sem + 7, corner_transfers(0) + [(f1x.at[0:104], xr.at[0:104], -1, 0)])
+        y_functionals(e1, 164, 16, 40, pl.ds(161, 16, stride=40), 0)
+        y_functionals(e1, 924, 1, 1, pl.ds(921, 1), 16)
+        f1 = f1 + send(sem + 10, [
             (f1y.at[0:3], yr.at[0:3], 0, -1),
             (f1y.at[3:7], yr.at[3:7], 0, 1),
         ])
-        if first:
-            f1 += send(sem + 4, x_after)
+        f0_columns = send(sem + 2, [(f0y.at[0:2], cr.at[0:2], 0, -1), (f0y.at[2:4], cr.at[2:4], 0, 1)])
 
         def y_level1(read):
             e = [read(j) for j in range(4)]
@@ -331,8 +327,6 @@
         f0 = send(sem, [
             (fq.at[0:97], qr.at[0:97], -1, 0),
             (fp.at[0:97], pr.at[0:97], 1, 0),
-            (f0y.at[0:2], cr.at[0:2], 0, -1),
-            (f0y.at[2:4], cr.at[2:4], 0, 1),
         ])
 
         if first:
@@ -388,23 +382,46 @@
         edge = [(3, tb) for tb in range(2)]
         inner_last = level1(inner)
 
-        def time_up1_pieces(pieces):
+        wait(f0_columns)
+        for tb in range(2):
+            t0[tb, pl.ds(64, 32, stride=72), :] = cr[tb, 0:32, :]
+            p, q = cr[2 + tb, 0:32, :], ROOT_THREE * f0y[tb, 0:32, :]
+            cb[tb, 2:34, :] = low_of(p, q)
+            cb[2 + tb, 2:34, :] = high_of(p, q)
+        edge_last = level1(edge)
+
+        def column_before(source, target):
+            for yb in range(2):
+                for tb in range(2):
+                    e = [cb[2 * yb + tb, source(j), :] for j in range(4)]
+                    p, q = p_of(e[0], e[1]), q_of(e[2], e[3])
+                    for xb in range(2):
+                        band = 4 * xb + 2 * yb + tb
+                        if band:
+                            value = high_of(p, q) if xb else low_of(p, q)
+                            c1[band - 1, target, :] = shrink(old(c1, band - 1, target, slice(None)) + value)
+
+        column_before(lambda j: pl.ds(2 + j, 15, stride=2), pl.ds(47, 15, stride=40))
+
+        def time_up1(b, pieces):
+            def band(tb):
+                if b == 0 and tb == 0:
+                    return [d1[40 + start : 40 + stop, :] for start, stop in pieces]
+                return [c1[2 * b - 1 + tb, start:stop, :] for start, stop in pieces]
+
+            values = jnp.concatenate([jnp.concatenate(band(tb), axis=0) for tb in range(2)], axis=1)
+            result = times(values, m1t)
+            n = 0
+            for start, stop in pieces:
+                for th in range(2):
+                    s1[th, b, start:stop, :] = result[n : n + stop - start, th * 128 : (th + 1) * 128]
+                n += stop - start
+
+        inner_rows = [(40, 240), (240, 440), (440, 640)]
+        end_rows = [(0, 40), (640, 680)]
+        for piece in inner_rows:
             for b in range(1, 4):
-                values = jnp.concatenate(
-                    [
-                        jnp.concatenate([c1[band, start:stop, :] for start, stop in pieces], axis=0)
-                        for band in (2 * b - 1, 2 * b)
-                    ],
-                    axis=1,
-                )
-                result = times(values, m1t)
-                n = 0
-                for start, stop in pieces:
-                    for th in range(2):
-                        s1[th, b, start:stop, :] = result[n : n + stop - start, th * 128 : (th + 1) * 128]
-                    n += stop - start
-
-        time_up1_pieces([(row * 40 + 8, row * 40 + 32) for row in range(1, 16)])
+                time_up1(b, [piece])
         wait(f1)
 
         for tile, first_row, count in ((0, 20, 3), (104, 0, 4)):
@@ -555,47 +572,8 @@
 
         loop(18, y_up2, unroll=6)
 
-        wait(f0)
-        for tb in range(2):
-            t0[tb, pl.ds(64, 32, stride=72), :] = cr[tb, 0:32, :]
-            corners = [fcr[number, n, used + tb : used + tb + 1, :] for n, (_, used) in enumerate(CORNERS)]
-            starts = []
-            for ref, low_row, corner in ((qr, 72, corners[0]), (pr, 176, corners[2])):
-                after = ROOT_THREE * corner
-                low, place, high = (ref, 31, 63) if tb else (xr, low_row + 31, 95)
-                low[place : place + 1, :] = low[place : place + 1, :] + RATIO * after
-                ref[high : high + 1, :] = ref[high : high + 1, :] + after
-                starts.append(ref[96:97, :] if tb else xr[low_row - 70 : low_row - 69, :])
-            for place, p, q, scale in (
-                (pl.ds(2, 32), cr[2 + tb, 0:32, :], ROOT_THREE * f0y[tb, 0:32, :], 1.0),
-                (pl.ds(0, 1), corners[3], starts[1], 1.0),
-                (pl.ds(34, 1), corners[1], starts[0], 1.0 / ROOT_THREE),
-            ):
-                cb[tb, place, :] = scale * low_of(p, q)
-                cb[2 + tb, place, :] = scale * high_of(p, q)
-        level1_ends(inner, inner_last)
-        level1_ends(edge, level1(edge))
-        for yb in range(2):
-            for tb in range(2):
-                e = [cb[2 * yb + tb, pl.ds(j, 17, stride=2), :] for j in range(4)]
-                p, q = p_of(e[0], e[1]), q_of(e[2], e[3])
-                for xb in range(2):
-                    band = 4 * xb + 2 * yb + tb
-                    if band:
-                        value = high_of(p, q) if xb else low_of(p, q)
-                        place = pl.ds(7, 17, stride=40)
-                        c1[band - 1, place, :] = shrink(old(c1, band - 1, place, slice(None)) + value)
-
-        time_up1_pieces([(0, 40), (640, 680)] + [(row * 40 + y, row * 40 + y + 8) for row in range(1, 16) for y in (0, 32)])
-
-        def time_up1(n):
-            place = rows(n * 136, 136)
-            lo = d1[rows(40 + n * 136, 136), :]
-            result = times(jnp.concatenate([lo, c1[0, place, :]], axis=1), m1t)
-            s1[0, 0, place, :] = result[:, :128]
-            s1[1, 0, place, :] = result[:, 128:]
-
-        loop(5, time_up1, unroll=5)
+        for piece in inner_rows:
+            time_up1(0, [piece])
 
         up_parts = [(chunk, th) for chunk in range(4) for th in range(2)]
 
@@ -626,21 +604,45 @@
                     n += 1
             return tuple(after)
 
-        def synthesis_half(first_k):
-            start = tuple(q_next(*one) for chunk, th in up_parts for one in y_up1(first_k, chunk, th))
-            lax.fori_loop(0, 8, functools.partial(up1, first_k), start, unroll=2)
-
-        return synthesis_half
-
-    synthesis = iteration(1, iteration(0, None))
-    synthesis(0)
-    synthesis(8)
+        def q_start(row):
+            return tuple(q_next(*one) for chunk, th in up_parts for one in y_up1(row, chunk, th))
+
+        lax.fori_loop(0, 14, functools.partial(up1, 1), q_start(1), unroll=2)
+        if not first:
+            loop(28, lambda n: finish(n + 2))
+
+        wait(f0)
+        for tb in range(2):
+            corners = [fcr[number, n, used + tb : used + tb + 1, :] for n, (_, used) in enumerate(CORNERS)]
+            starts = []
+            for ref, low_row, corner in ((qr, 72, corners[0]), (pr, 176, corners[2])):
+                after = ROOT_THREE * corner
+                low, place, high = (ref, 31, 63) if tb else (xr, low_row + 31, 95)
+                low[place : place + 1, :] = low[place : place + 1, :] + RATIO * after
+                ref[high : high + 1, :] = ref[high : high + 1, :] + after
+                starts.append(ref[96:97, :] if tb else xr[low_row - 70 : low_row - 69, :])
+            for place, p, q, scale in (
+                (pl.ds(0, 1), corners[3], starts[1], 1.0),
+                (pl.ds(34, 1), corners[1], starts[0], 1.0 / ROOT_THREE),
+            ):
+                cb[tb, place, :] = scale * low_of(p, q)
+                cb[2 + tb, place, :] = scale * high_of(p, q)
+        level1_ends(inner, inner_last)
+        level1_ends(edge, edge_last)
+        column_before(lambda j: pl.ds(j, 2, stride=32), pl.ds(7, 2, stride=640))
+        for b in range(4):
+            time_up1(b, end_rows)
+        up1(0, 0, q_start(0))
+        up1(15, 0, q_start(15))
 
     def finish(r):
         for th in range(2):
             out[r, :, th * 128 : (th + 1) * 128] = reb[th, rows(r * 64, 64), :]
 
-    loop(32, finish, unroll=2)
+    iteration(0)
+    iteration(1)
+    for r in (0, 1, 30, 31):
+        finish(r)
 
 
 def solution(mesh):
@@ -653,7 +655,7 @@
         return pltpu.VMEM(shape, BF16)
 
     scratch = [
-        pltpu.VMEM((32, 64, 256), jnp.int32),
+        pltpu.VMEM((32, 64, 256), jnp.int32), v(2048, 256), v(2048, 256),
         b(768, 256), b(768, 256), b(384, 128), b(384, 128), b(384, 128), b(384, 128),
         v(2, 32 * 72, 128), v(7, 17 * 40, 128), v(24 * 40, 128),
         v(22 * 40, 128), v(2, 12 * 40, 128), v(4, 10 * 24, 128), v(12 * 24, 128),

time: 27.7 us -> 26.4 us (0.953)
  Pallas kernels: 26.2 us -> 24.9 us
    pallas_call x1, Pallas kernels: 26.2 us -> 24.9 us  [on_device(): pl.pallas_call(functools.partial(kernel, nx, ny), out_shape=jax.ShapeDtyp...]
where the time goes in v4:
time: 26.4 us; the launch traced here: 26.3 us
  Pallas kernels  24.9 us (94%)
  local copies, waits for them, and re-layouts  1.32 us (5%)
    pallas_call x1, Pallas kernels, on_device(): pl.pallas_call(functools.partial(kernel, nx, ny), out_shape=jax.ShapeDtyp...  24.9 us
    unnamed x1, local copies, waits for them, and re-layouts  1.32 us

profile of v4, /device:TPU:0, one launch (start us, length us, event | category | flops | bytes accessed | tf_op | source)
XLA Modules:
  0.0 26.3 jit_solution(1457507196166983764)
XLA Ops:
  0.0 24.9 %shard_map.17 = f32[32,64,256]{2,1,0:T(8,128)S(1)} custom-call(s32[32,64,256]{2,1,0:T(8,128)} %counts_hbm.1), custom_call_target="tpu_custom_call" | custom-call | tf_op jit(solution)/shard_map/pallas_call | solution.py:672
  24.9 1.3 %copy.3 = f32[32,64,256]{2,1,0:T(8,128)} copy(f32[32,64,256]{2,1,0:T(8,128)S(1)} %shard_map.17) | data formatting | bytes 4194304

commit v5 on v4

--- a/solution.py
+++ b/solution.py
@@ -133,7 +133,7 @@
     for dx, dy in around:
         pl.semaphore_signal(barrier, inc=1, device_id=device(dx, dy), device_id_type=MESH)
 
-    def send(first_sem, transfers):
+    def send(first_sem, transfers, start=True):
         copies = []
         for n, (source, target, dx, dy) in enumerate(transfers):
             copy = pltpu.make_async_remote_copy(
@@ -144,7 +144,8 @@
                 device_id=device(dx, dy),
                 device_id_type=MESH,
             )
-            copy.start()
+            if start:
+                copy.start()
             copies.append(copy)
         return copies
 
@@ -301,8 +302,19 @@
         corner_level1(0, f0q)
         if first:
             pl.semaphore_wait(barrier, 8)
-            f1 = send(sem + 4, after_transfers)
-        f1 = f1 + send(sem + 7, corner_transfers(0) + [(f1x.at[0:104], xr.at[0:104], -1, 0)])
+            f1 = send(sem + 4, after_transfers, start=False)
+        f1_before = send(
+            sem + 7, corner_transfers(0) + [(f1x.at[0:104], xr.at[0:104], -1, 0)], start=not first
+        )
+        if first:
+
+            def start_all(copies):
+                for copy in copies:
+                    copy.start()
+
+            pl.when(gx == 0)(lambda: start_all(f1_before[:2] + f1[:2] + f1_before[2:] + f1[2:]))
+            pl.when(gx != 0)(lambda: start_all(f1[:2] + f1_before[:2] + f1[2:] + f1_before[2:]))
+        f1 = f1 + f1_before
         y_functionals(e1, 164, 16, 40, pl.ds(161, 16, stride=40), 0)
         y_functionals(e1, 924, 1, 1, pl.ds(921, 1), 16)
         f1 = f1 + send(sem + 10, [
@@ -611,36 +623,39 @@
         if not first:
             loop(28, lambda n: finish(n + 2))
 
-        wait(f0)
-        for tb in range(2):
-            corners = [fcr[number, n, used + tb : used + tb + 1, :] for n, (_, used) in enumerate(CORNERS)]
-            starts = []
-            for ref, low_row, corner in ((qr, 72, corners[0]), (pr, 176, corners[2])):
-                after = ROOT_THREE * corner
-                low, place, high = (ref, 31, 63) if tb else (xr, low_row + 31, 95)
-                low[place : place + 1, :] = low[place : place + 1, :] + RATIO * after
-                ref[high : high + 1, :] = ref[high : high + 1, :] + after
-                starts.append(ref[96:97, :] if tb else xr[low_row - 70 : low_row - 69, :])
-            for place, p, q, scale in (
-                (pl.ds(0, 1), corners[3], starts[1], 1.0),
-                (pl.ds(34, 1), corners[1], starts[0], 1.0 / ROOT_THREE),
-            ):
-                cb[tb, place, :] = scale * low_of(p, q)
-                cb[2 + tb, place, :] = scale * high_of(p, q)
-        level1_ends(inner, inner_last)
-        level1_ends(edge, edge_last)
-        column_before(lambda j: pl.ds(j, 2, stride=32), pl.ds(7, 2, stride=640))
-        for b in range(4):
-            time_up1(b, end_rows)
-        up1(0, 0, q_start(0))
-        up1(15, 0, q_start(15))
+        def ends():
+            wait(f0)
+            for tb in range(2):
+                corners = [fcr[number, n, used + tb : used + tb + 1, :] for n, (_, used) in enumerate(CORNERS)]
+                starts = []
+                for ref, low_row, corner in ((qr, 72, corners[0]), (pr, 176, corners[2])):
+                    after = ROOT_THREE * corner
+                    low, place, high = (ref, 31, 63) if tb else (xr, low_row + 31, 95)
+                    low[place : place + 1, :] = low[place : place + 1, :] + RATIO * after
+                    ref[high : high + 1, :] = ref[high : high + 1, :] + after
+                    starts.append(ref[96:97, :] if tb else xr[low_row - 70 : low_row - 69, :])
+                for place, p, q, scale in (
+                    (pl.ds(0, 1), corners[3], starts[1], 1.0),
+                    (pl.ds(34, 1), corners[1], starts[0], 1.0 / ROOT_THREE),
+                ):
+                    cb[tb, place, :] = scale * low_of(p, q)
+                    cb[2 + tb, place, :] = scale * high_of(p, q)
+            level1_ends(inner, inner_last)
+            level1_ends(edge, edge_last)
+            column_before(lambda j: pl.ds(j, 2, stride=32), pl.ds(7, 2, stride=640))
+            for b in range(4):
+                time_up1(b, end_rows)
+            up1(0, 0, q_start(0))
+            up1(15, 0, q_start(15))
+
+        return ends
 
     def finish(r):
         for th in range(2):
             out[r, :, th * 128 : (th + 1) * 128] = reb[th, rows(r * 64, 64), :]
 
-    iteration(0)
-    iteration(1)
+    iteration(0)()
+    iteration(1)()
     for r in (0, 1, 30, 31):
         finish(r)
 

time: 26.4 us -> 26.3 us (level)
  no operation moved by 1% of the time
where the time goes in v5:
time: 26.3 us; the launch traced here: 26.1 us
  Pallas kernels  24.8 us (94%)
  local copies, waits for them, and re-layouts  1.32 us (5%)
    pallas_call x1, Pallas kernels, on_device(): pl.pallas_call(functools.partial(kernel, nx, ny), out_shape=jax.ShapeDtyp...  24.8 us
    unnamed x1, local copies, waits for them, and re-layouts  1.32 us

profile of v5, /device:TPU:0, one launch (start us, length us, event | category | flops | bytes accessed | tf_op | source)
XLA Modules:
  0.0 26.1 jit_solution(17870984365300188269)
XLA Ops:
  0.0 24.8 %shard_map.17 = f32[32,64,256]{2,1,0:T(8,128)S(1)} custom-call(s32[32,64,256]{2,1,0:T(8,128)} %counts_hbm.1), custom_call_target="tpu_custom_call" | custom-call | tf_op jit(solution)/shard_map/pallas_call | solution.py:687
  24.8 1.3 %copy.3 = f32[32,64,256]{2,1,0:T(8,128)} copy(f32[32,64,256]{2,1,0:T(8,128)S(1)} %shard_map.17) | data formatting | bytes 4194304

commit v6 on v5

--- a/solution.py
+++ b/solution.py
@@ -582,7 +582,7 @@
             d1[pl.ds(r * 40 + 6, 17, stride=2), :] = even
             d1[pl.ds(r * 40 + 7, 17, stride=2), :] = odd
 
-        loop(18, y_up2, unroll=6)
+        loop(17, lambda r: y_up2(r + 1), unroll=17)
 
         for piece in inner_rows:
             time_up1(0, [piece])

time: 26.3 us -> 26 us (0.989)
  Pallas kernels: 24.8 us -> 24.5 us
    pallas_call x1, Pallas kernels: 24.8 us -> 24.5 us  [on_device(): pl.pallas_call(functools.partial(kernel, nx, ny), out_shape=jax.ShapeDtyp...]
where the time goes in v6:
time: 26 us; the launch traced here: 25.9 us
  Pallas kernels  24.5 us (94%)
  local copies, waits for them, and re-layouts  1.32 us (5%)
    pallas_call x1, Pallas kernels, on_device(): pl.pallas_call(functools.partial(kernel, nx, ny), out_shape=jax.ShapeDtyp...  24.5 us
    unnamed x1, local copies, waits for them, and re-layouts  1.32 us

profile of v6, /device:TPU:0, one launch (start us, length us, event | category | flops | bytes accessed | tf_op | source)
XLA Modules:
  0.0 25.9 jit_solution(18104796141816976890)
XLA Ops:
  0.0 24.5 %shard_map.17 = f32[32,64,256]{2,1,0:T(8,128)S(1)} custom-call(s32[32,64,256]{2,1,0:T(8,128)} %counts_hbm.1), custom_call_target="tpu_custom_call" | custom-call | tf_op jit(solution)/shard_map/pallas_call | solution.py:687
  24.5 1.3 %copy.3 = f32[32,64,256]{2,1,0:T(8,128)} copy(f32[32,64,256]{2,1,0:T(8,128)S(1)} %shard_map.17) | data formatting | bytes 4194304
